TPU v7x, 128 devices: a whole 4x4x4 slice. The times are simulated.
128 devices in a mesh: row: 4 (over y), col: 8 (over x_hi, z), ch: 4 (over x_lo, core).
Axes of the slice: x: 4 (x_hi: 2, x_lo: 2; x = x_hi * 2 + x_lo), y: 4, z: 4, core: 2. Of those that a mesh axis runs over, the one named last changes fastest.
Arguments:
- pair_tensor: bfloat16 [128, 1024, 1024], P('ch', 'row', 'col'), may hold values from -6 to 6
- token_mask: int32 [1024], replicated, may hold values 0 or 1
- norm_in_gain: float32 [128], replicated, may hold values from 0.5 to 1.5
- norm_in_bias: float32 [128], replicated, may hold values from -3 to 3
- proj_in: bfloat16 [128, 256], replicated, may hold values from -0.5 to 0.5
- gate_in: bfloat16 [128, 256], replicated, may hold values from -0.5 to 0.5
- norm_out_gain: float32 [128], replicated, may hold values from 0.5 to 1.5
- norm_out_bias: float32 [128], replicated, may hold values from -3 to 3
- proj_out: bfloat16 [128, 128], replicated, may hold values from -0.5 to 0.5
- gate_out: bfloat16 [128, 128], replicated, may hold values from -0.5 to 0.5
Outputs:
- update: bfloat16 [128, 1024, 1024], P('ch', 'row', 'col')
All inputs are finite; a program needn't handle non-finite values.
Results may differ from a plain program's by a relative error of at most 0.005.
Values may be sent and summed in bfloat16 or wider, within the bound.
A program may use at most 192 MiB of HBM per device.

v0:
```python
import jax
import jax.numpy as jnp
from jax import lax
from jax.sharding import PartitionSpec as P

epsilon = 1e-05


def channel_norm(values, gain_vec, bias_vec):
    center = jnp.mean(values, axis=0, keepdims=True)
    second = jnp.mean(values * values, axis=0, keepdims=True)
    spread = second - center * center
    return (values - center) * lax.rsqrt(spread + epsilon) * gain_vec[:, None, None] + bias_vec[
        :, None, None
    ]


def local(
    pair_tensor,
    token_mask,
    norm_in_gain,
    norm_in_bias,
    proj_in,
    gate_in,
    norm_out_gain,
    norm_out_bias,
    proj_out,
    gate_out,
):
    chan_part = pair_tensor.shape[0]
    row_count = pair_tensor.shape[1]
    col_count = pair_tensor.shape[2]
    width_hid = proj_out.shape[0]
    ch_parts = lax.axis_size("ch")
    hid_part = width_hid // ch_parts
    my_ch = lax.axis_index("ch")
    row_start = lax.axis_index("row") * row_count
    col_start = lax.axis_index("col") * col_count
    hid_start = my_ch * hid_part
    full_pair = lax.all_gather(pair_tensor, "ch", axis=0, tiled=True)
    normed = channel_norm(full_pair.astype(jnp.float32), norm_in_gain, norm_in_bias).astype(
        jnp.bfloat16
    )
    row_mask = lax.dynamic_slice_in_dim(token_mask, row_start, row_count, 0).astype(jnp.float32)
    col_mask = lax.dynamic_slice_in_dim(token_mask, col_start, col_count, 0).astype(jnp.float32)
    pair_mask = row_mask[:, None] * col_mask[None, :]
    proj_cols = jnp.concatenate(
        [
            lax.dynamic_slice_in_dim(proj_in, hid_start, hid_part, 1),
            lax.dynamic_slice_in_dim(proj_in, width_hid + hid_start, hid_part, 1),
        ],
        axis=1,
    )
    gate_cols = jnp.concatenate(
        [
            lax.dynamic_slice_in_dim(gate_in, hid_start, hid_part, 1),
            lax.dynamic_slice_in_dim(gate_in, width_hid + hid_start, hid_part, 1),
        ],
        axis=1,
    )
    proj_val = jnp.einsum("cik,ch->hik", normed, proj_cols, preferred_element_type=jnp.float32)
    gate_val = jnp.einsum("cik,ch->hik", normed, gate_cols, preferred_element_type=jnp.float32)
    hidden_act = (jax.nn.sigmoid(gate_val) * proj_val * pair_mask[None, :, :]).astype(jnp.bfloat16)
    left_act = hidden_act[:hid_part]
    right_act = hidden_act[hid_part:]
    right_all = lax.all_gather(right_act, "row", axis=1, tiled=True)
    right_mine = lax.all_to_all(right_all, "col", split_axis=1, concat_axis=2, tiled=True)
    tri_sum = jnp.einsum(
        "hik,hjk->hij",
        lax.all_gather(left_act, "col", axis=2, tiled=True),
        right_mine,
        preferred_element_type=jnp.float32,
    )
    first_sum = jnp.sum(tri_sum, axis=0, keepdims=True)
    square_sum = jnp.sum(tri_sum * tri_sum, axis=0, keepdims=True)
    first_all, square_all = lax.psum((first_sum, square_sum), "ch")
    center = first_all / width_hid
    spread = square_all / width_hid - center * center
    gain_part = lax.dynamic_slice_in_dim(norm_out_gain, hid_start, hid_part, 0)
    bias_part = lax.dynamic_slice_in_dim(norm_out_bias, hid_start, hid_part, 0)
    tri_norm = (
        (tri_sum - center) * lax.rsqrt(spread + epsilon) * gain_part[:, None, None]
        + bias_part[:, None, None]
    ).astype(jnp.bfloat16)
    proj_rows = lax.dynamic_slice_in_dim(proj_out, hid_start, hid_part, 0)
    partial_out = jnp.einsum("hij,hc->cij", tri_norm, proj_rows, preferred_element_type=jnp.float32)
    summed_out = lax.psum_scatter(partial_out, "ch", scatter_dimension=0, tiled=True)
    gate_cols_out = lax.dynamic_slice_in_dim(gate_out, my_ch * chan_part, chan_part, 1)
    out_gate = jnp.einsum("dij,dc->cij", normed, gate_cols_out, preferred_element_type=jnp.float32)
    return (jax.nn.sigmoid(out_gate) * summed_out).astype(jnp.bfloat16)


def solution(mesh):
    in_specs = (P("ch", "row", "col"), P(), P(), P(), P(), P(), P(), P(), P(), P())
    out_specs = P("ch", "row", "col")
    return jax.shard_map(local, mesh=mesh, in_specs=in_specs, out_specs=out_specs, check_vma=False)
```

profile of v0, /device:TPU:1, one launch (start us, length us, event | category | flops | bytes accessed | tf_op | source)
XLA Modules:
  0.0 715.8 jit_solution(15431415426631083561)
XLA Ops:
  6.5 0.0 copy-start
  6.5 0.0 all-gather.4.cloned.1.call-start
  6.5 0.7 all-gather.4.cloned.1.call-update
  7.3 0.0 all-gather.8.cloned.1.call-start
  7.3 0.9 constant_dynamic-slice_fusion.1
  8.2 0.1 copy.38
  8.3 0.1 copy.39
  8.4 0.1 copy.36
  8.5 0.1 copy.37
  8.6 0.8 dynamic-slice_convert_fusion.1
  9.4 0.8 dynamic-slice_convert_fusion
  10.1 0.1 broadcast_multiply_fusion
  10.2 83.8 %all-gather.4.cloned.1.call-done = bf16[128,256,128]{2,1,0:T(8,128)(2,1)} async-done(((bf16[32,256,128]{2,1,0:T(8,128)(2,1)}), bf16[128,256,128]{2,1,0:T(8,128)(2,1)}) %all-gather.4.cloned.1.call-update) | async-done | bytes 8388624 | tf_op jit(solution)/shard_map/all_gather | solution.py:40
  94.1 5.8 convert_reduce_fusion
  99.9 0.0 copy-done.4
  99.9 0.0 copy-done.3
  99.9 0.0 copy-done.2
  99.9 4.3 fusion.3
  104.2 0.0 copy-start.1
  104.2 5.6 fusion.7
  109.8 0.0 copy-done.1
  109.8 19.5 %multiply_convert_fusion = bf16[64,256,128]{2,0,1:T(8,128)(2,1)S(1)} fusion(f32[64,256,128]{2,0,1:T(8,128)S(1)} %fusion.7, f32[256,128]{1,0:T(8,128)S(1)} %broadcast_multiply_fusion, bf16[128,256,128]{2,1,0:T(8,128)(2,1)S(1)} %fusion.3, bf16[128,32]{0,1:T(8,128)(2,1)S(1)} %copy.37, bf16[128,32]{0,1:T(8,128)(2,1)S(1)} %copy.36), kind=kOutput, calls=%fused_computation.11 | convolution fusion | flops 549486592 | bytes 21118976 | tf_op jit(solution)/shard_map/cik,ch->hik/dot_general | solution.py:62
  129.3 2.8 fusion.32
  132.1 0.0 all-gather.8.cloned.1.call-update
  132.1 0.0 all-gather.6.cloned.1.call-start
  132.2 0.7 all-gather.6.cloned.1.call-update
  132.8 0.0 all-reduce.3.cloned.1.call-start
  132.9 82.9 %all-gather.8.cloned.1.call-done = bf16[32,1024,128]{2,0,1:T(8,128)(2,1)} async-done(((bf16[32,256,128]{2,0,1:T(8,128)(2,1)}), bf16[32,1024,128]{2,0,1:T(8,128)(2,1)}) %all-gather.8.cloned.1.call-update) | async-done | bytes 8388624 | tf_op jit(solution)/shard_map/all_gather | solution.py:66
  215.8 124.0 %all_to_all.18 = bf16[32,1024,128]{2,0,1:T(8,128)(2,1)} all-to-all(bf16[32,1024,128]{2,0,1:T(8,128)(2,1)} %all-gather.8.cloned.1.call-done), channel_id=1, replica_groups=mesh['row'=4,'col'=8,'ch'=4] {'col'}, dimensions={1} | all-to-all | bytes 16777216 | tf_op jit(solution)/shard_map/all_to_all | solution.py:67
  339.8 12.1 %copy.57 = bf16[32,8,128,128]{3,1,2,0:T(8,128)(2,1)} copy(bf16[32,8,128,128]{3,0,2,1:T(8,128)(2,1)} %bitcast.26) | data formatting | bytes 16777216 | tf_op jit(solution)/shard_map/all_to_all | solution.py:67
  351.9 13.4 %all_to_all.16 = bf16[32,128,1024]{2,1,0:T(8,128)(2,1)} reshape(bf16[32,128,8,128]{3,2,1,0:T(8,128)(2,1)} %bitcast.27) | data formatting | bytes 16777216 | tf_op jit(solution)/shard_map/all_to_all | solution.py:67
  365.3 115.1 %all-gather.6.cloned.1.call-done = bf16[32,256,1024]{2,0,1:T(8,128)(2,1)} async-done(((bf16[32,256,128]{2,0,1:T(8,128)(2,1)}), bf16[32,256,1024]{2,0,1:T(8,128)(2,1)}) %all-gather.6.cloned.1.call-update) | async-done | bytes 16777232 | tf_op jit(solution)/shard_map/all_gather | solution.py:70
  480.5 21.5 %fusion.31 = (f32[256,128]{1,0:T(8,128)}, f32[256,128]{1,0:T(8,128)}, f32[32,256,128]{2,1,0:T(8,128)}) fusion(bf16[32,128,1024]{2,1,0:T(8,128)(2,1)} %all_to_all.16, bf16[32,256,1024]{2,0,1:T(8,128)(2,1)} %all-gather.6.cloned.1.call-done), kind=kOutput, calls=%fused_computation.48 | convolution fusion | flops 2150563840 | bytes 29622272 | tf_op jit(solution)/shard_map/hik,hjk->hij/dot_general | solution.py:68
  502.0 0.0 all-reduce.3.cloned.1.call-update
  502.0 0.3 reduce-scatter.2.cloned.1.call-start
  502.3 0.0 copy-done.6
  502.3 0.1 dynamic_slice.38
  502.3 0.0 copy-done.7
  502.3 0.1 dynamic_slice.39
  502.4 34.7 %all-reduce.3.cloned.1.call-done = (f32[1,256,128]{2,1,0:T(8,128)}, f32[1,256,128]{2,1,0:T(8,128)}) async-done(((f32[1,256,128]{2,1,0:T(8,128)}, f32[1,256,128]{2,1,0:T(8,128)}), (f32[1,256,128]{2,1,0:T(8,128)}, f32[1,256,128]{2,1,0:T(8,128)})) %all-reduce.3.cloned.1.call-update) | async-done | bytes 262160 | tf_op jit(solution)/shard_map/psum | solution.py:76
  537.2 1.0 multiply_bitcast_fusion
  538.2 3.0 add_convert_fusion
  541.2 0.0 copy-done
  541.2 8.1 %fusion.17 = f32[128,256,128]{2,0,1:T(8,128)} fusion(bf16[32,256,128]{2,1,0:T(8,128)(2,1)S(1)} %add_convert_fusion, bf16[128,128]{1,0:T(8,128)(2,1)S(1)} %copy-done, s32[]{:T(128)S(6)} %select_n.20), kind=kOutput, calls=%fused_computation.21 | convolution fusion | flops 268435456 | bytes 18882564 | tf_op jit(solution)/shard_map/hij,hc->cij/dot_general | solution.py:86
  549.3 0.0 reduce-scatter.2.cloned.1.call-update
  549.4 147.3 %reduce-scatter.2.cloned.1.call-done = f32[32,256,128]{2,0,1:T(8,128)} async-done(((f32[128,256,128]{2,0,1:T(8,128)}), f32[32,256,128]{2,0,1:T(8,128)}) %reduce-scatter.2.cloned.1.call-update) | async-done | bytes 4194320 | tf_op jit(solution)/shard_map/reduce_scatter | solution.py:87
  696.7 10.2 %multiply_convert_fusion.1 = bf16[32,256,128]{2,0,1:T(8,128)(2,1)S(1)} fusion(f32[32,256,128]{2,0,1:T(8,128)} %reduce-scatter.2.cloned.1.call-done, bf16[128,256,128]{2,1,0:T(8,128)(2,1)} %copy-done.1, bf16[128,128]{1,0:T(8,128)(2,1)S(1)} %copy-done.5, s32[]{:T(128)S(6)} %select_n.20), kind=kOutput, calls=%fused_computation.18 | convolution fusion | flops 273678336 | bytes 14712836 | tf_op jit(solution)/shard_map/dij,dc->cij/dot_general | solution.py:89
  706.9 2.1 copy.34
  (8 shorter events, 0.0 us)
Async XLA Ops:
  6.5 534.7 %copy-start = (bf16[128,128]{1,0:T(8,128)(2,1)S(1)}, bf16[128,128]{1,0:T(8,128)(2,1)}, u32[]{:S(2)}) copy-start(bf16[128,128]{1,0:T(8,128)(2,1)} %param.18) | copy-start | bytes 98308
  6.5 93.4 %copy-start.4 = (f32[128]{0:T(128)S(1)}, f32[128]{0:T(128)}, u32[]{:S(2)}) copy-start(f32[128]{0:T(128)} %param.12) | copy-start | bytes 1540
  6.5 93.4 %copy-start.3 = (f32[128]{0:T(128)S(1)}, f32[128]{0:T(128)}, u32[]{:S(2)}) copy-start(f32[128]{0:T(128)} %param.13) | copy-start | bytes 1540
  6.5 87.5 %all-gather.4.cloned.1.call-start = ((), (), s32[]{:S(2)}) async-start(), calls=%async_computation.2 | async-start | bytes 10485760 | tf_op jit(solution)/shard_map/all_gather | solution.py:40
  7.3 208.6 %all-gather.8.cloned.1.call-start = ((), (), s32[]{:S(2)}) async-start(), calls=%async_computation.4 | async-start | bytes 10485760 | tf_op jit(solution)/shard_map/all_gather | solution.py:66
  94.1 5.8 copy-start.2
  104.2 5.6 copy-start.1
  132.1 348.3 %all-gather.6.cloned.1.call-start = ((), (), s32[]{:S(2)}) async-start(), calls=%async_computation.3 | async-start | bytes 18874368 | tf_op jit(solution)/shard_map/all_gather | solution.py:70
  132.8 404.3 %all-reduce.3.cloned.1.call-start = ((), (), s32[]{:S(2)}) async-start(), calls=%async_computation.6 | async-start | bytes 524288 | tf_op jit(solution)/shard_map/psum | solution.py:76
  365.3 136.9 %copy-start.6 = (f32[128]{0:T(128)S(1)}, f32[128]{0:T(128)}, u32[]{:S(2)}) copy-start(f32[128]{0:T(128)} %param.16) | copy-start | bytes 1540
  365.3 137.0 %copy-start.7 = (f32[128]{0:T(128)S(1)}, f32[128]{0:T(128)}, u32[]{:S(2)}) copy-start(f32[128]{0:T(128)} %param.17) | copy-start | bytes 1540
  502.0 194.7 %reduce-scatter.2.cloned.1.call-start = ((), (), s32[]{:S(2)}) async-start(), calls=%async_computation.5 | async-start | bytes 20971520 | tf_op jit(solution)/shard_map/reduce_scatter | solution.py:87
  549.3 147.4 %copy-start.5 = (bf16[128,128]{1,0:T(8,128)(2,1)S(1)}, bf16[128,128]{1,0:T(8,128)(2,1)}, u32[]{:S(2)}) copy-start(bf16[128,128]{1,0:T(8,128)(2,1)} %param.19) | copy-start | bytes 98308
Sparse Core Ops, SparseCore 0:
  9.0 85.0 all-gather.3
  132.2 83.5 all-gather.7
  218.0 262.3 all-gather.5
  502.1 34.9 all-reduce.2
  549.5 147.1 reduce-scatter.1
where the time goes:
time: 723 us; the launch traced here: 716 us
  waiting for transfers between devices  465 us (64%)
  blocking collectives  124 us (17%)
  matrix products  64.9 us (9%)
  local copies, waits for them, and re-layouts  31.9 us (4%)
  other arithmetic  15.8 us (2%)
  between operations  13.5 us (2%)
    reduce_scatter x1, waiting for transfers between devices, local(): lax.psum_scatter(partial_out, 'ch', scatter_dimension=0, tiled=True)  147 us
    all_to_all x1, blocking collectives, local(): lax.all_to_all(right_all, 'col', split_axis=1, concat_axis=2, tiled=True)  124 us
    all_gather x1, waiting for transfers between devices, local(): lax.all_gather(left_act, 'col', axis=2, tiled=True)  115 us
    all_gather x1, waiting for transfers between devices, local(): full_pair = lax.all_gather(pair_tensor, 'ch', axis=0, tiled=True)  83.8 us
    all_gather x1, waiting for transfers between devices, local(): right_all = lax.all_gather(right_act, 'row', axis=1, tiled=True)  82.9 us
    psum x1, waiting for transfers between devices, local(): first_all, square_all = lax.psum((first_sum, square_sum), 'ch')  34.7 us
    all_to_all x2, local copies, waits for them, and re-layouts, local(): lax.all_to_all(right_all, 'col', split_axis=1, concat_axis=2, tiled=True)  25.5 us
    dot_general x1, matrix products, local(): jnp.einsum('hik,hjk->hij', lax.all_gather(left_act, 'col', axis=2, tiled=...  21.5 us
  transfers between devices with their start and end apart: 5, of which 5 were waited for; matrix products, arithmetic and copies ran while one was open for 2% of the time, Pallas kernels for 0%

commit v1 on v0

v1 whole, which is shorter than its diff:
```python
import functools

import jax
import jax.numpy as jnp
from jax import lax
from jax.experimental import pallas as pl
from jax.experimental.pallas import tpu as pltpu
from jax.sharding import PartitionSpec as P

epsilon = 1e-05
WORLD = ("row", "col", "ch")
STEP = 16


def norm_rows(values, gain, bias):
    width = values.shape[0]
    center = jnp.sum(values, axis=0, keepdims=True) * (1.0 / width)
    second = jnp.sum(values * values, axis=0, keepdims=True) * (1.0 / width)
    spread = second - center * center
    return ((values - center) * lax.rsqrt(spread + epsilon) * gain + bias).astype(jnp.bfloat16)


def sigmoid(values):
    return 0.5 * jnp.tanh(0.5 * values) + 0.5


def hidden_kernel(pair_ref, mask_ref, gain_ref, bias_ref, weight_ref, hid_ref, gate_ref, flat, acts):
    chans, _, lanes = pair_ref.shape
    hid2 = 2 * hid_ref.shape[0]
    flat[...] = pair_ref[...].astype(jnp.float32).reshape(chans * STEP, lanes)
    gain, bias = gain_ref[...], bias_ref[...]
    weight = weight_ref[...]
    for i in range(0, STEP, 2):
        both = [norm_rows(flat[pl.ds(i + d, chans, stride=STEP), :], gain, bias) for d in range(2)]
        prod = jnp.dot(weight, jnp.concatenate(both, axis=1), preferred_element_type=jnp.float32)
        for d in range(2):
            part = prod[:, d * lanes : (d + 1) * lanes]
            act = sigmoid(part[:hid2]) * part[hid2 : 2 * hid2] * mask_ref[i + d : i + d + 1, :]
            acts[pl.ds(i + d, hid2, stride=STEP), :] = act
            gate_ref[i + d] = sigmoid(part[2 * hid2 :])
    rounded = acts[...].astype(jnp.bfloat16).reshape(hid2, STEP, lanes)
    hid_ref[:, 0] = rounded[: hid2 // 2]
    hid_ref[:, 1] = rounded[hid2 // 2 :]


def triangle_kernel(recv_ref, out_ref, left, right):
    rows, cols, chs, _, tall, lanes = recv_ref.shape
    for r in range(rows):
        for h in range(chs):
            for c in range(cols):
                at = (pl.ds((r * chs + h) * tall, tall), pl.ds(c * lanes, lanes))
                left[at] = recv_ref[r, c, h, 0]
                right[at] = recv_ref[r, c, h, 1]
    for r in range(rows):
        prod = lax.dot_general(
            left[pl.ds(r * chs * tall, chs * tall), :],
            right[...],
            (((1,), (1,)), ((), ())),
            preferred_element_type=jnp.float32,
        ).astype(jnp.bfloat16)
        for h in range(chs):
            for c in range(cols):
                out_ref[r, c, h] = prod[h * tall : (h + 1) * tall, c * lanes : (c + 1) * lanes]


def update_kernel(tri_ref, gate_ref, gain_ref, bias_ref, weight_ref, out_ref, flat, outs):
    hids, _, lanes = tri_ref.shape
    chans = out_ref.shape[0]
    flat[...] = tri_ref[...].astype(jnp.float32).reshape(hids * STEP, lanes)
    gain, bias = gain_ref[...], bias_ref[...]
    weight = weight_ref[...]
    for i in range(0, STEP, 2):
        both = [norm_rows(flat[pl.ds(i + d, hids, stride=STEP), :], gain, bias) for d in range(2)]
        prod = jnp.dot(weight, jnp.concatenate(both, axis=1), preferred_element_type=jnp.float32)
        for d in range(2):
            outs[pl.ds(i + d, chans, stride=STEP), :] = gate_ref[i + d] * prod[:, d * lanes : (d + 1) * lanes]
    out_ref[...] = outs[...].astype(jnp.bfloat16).reshape(chans, STEP, lanes)


def whole(shape):
    return pl.BlockSpec(shape, lambda i: (0,) * len(shape))


def local(pair, token_mask, gain_in, bias_in, proj_in, gate_in, gain_out, bias_out, proj_out, gate_out):
    chan_part, row_count, lanes = pair.shape
    rows, cols, chs = (lax.axis_size(a) for a in WORLD)
    chans, hids = chan_part * chs, proj_out.shape[0]
    world = rows * cols * chs
    tall = row_count // chs
    row_start = lax.axis_index("row") * row_count + lax.axis_index("ch") * tall
    col_start = lax.axis_index("col") * lanes
    row_mask = lax.dynamic_slice_in_dim(token_mask, row_start, tall, 0).astype(jnp.float32)
    col_mask = lax.dynamic_slice_in_dim(token_mask, col_start, lanes, 0).astype(jnp.float32)
    mask = row_mask[:, None] * col_mask[None, :]
    wide = lambda v: jnp.broadcast_to(v[:, None], (v.shape[0], lanes))
    weight = jnp.concatenate([gate_in, proj_in, gate_out], axis=1).T
    params = pltpu.CompilerParams(vmem_limit_bytes=48 * 2**20)

    mine = lax.all_to_all(pair, "ch", 1, 0, tiled=True)
    hid, gate = pl.pallas_call(
        hidden_kernel,
        name="hidden",
        grid=(tall // STEP,),
        out_shape=(
            jax.ShapeDtypeStruct((hids, 2, tall, lanes), jnp.bfloat16),
            jax.ShapeDtypeStruct((tall, chans, lanes), jnp.float32),
        ),
        in_specs=[
            pl.BlockSpec((chans, STEP, lanes), lambda i: (0, i, 0)),
            pl.BlockSpec((STEP, lanes), lambda i: (i, 0)),
            whole((chans, lanes)),
            whole((chans, lanes)),
            whole(weight.shape),
        ],
        out_specs=(
            pl.BlockSpec((hids, 2, STEP, lanes), lambda i: (0, 0, i, 0)),
            pl.BlockSpec((STEP, chans, lanes), lambda i: (i, 0, 0)),
        ),
        scratch_shapes=[
            pltpu.VMEM((chans * STEP, lanes), jnp.float32),
            pltpu.VMEM((2 * hids * STEP, lanes), jnp.float32),
        ],
        compiler_params=params,
    )(mine, mask, wide(gain_in), wide(bias_in), weight)
    recv = lax.all_to_all(hid, WORLD, 0, 0, tiled=True).reshape(rows, cols, chs, 2, tall, lanes)
    tri = pl.pallas_call(
        triangle_kernel,
        name="triangle",
        out_shape=jax.ShapeDtypeStruct((rows, cols, chs, tall, lanes), jnp.bfloat16),
        scratch_shapes=[pltpu.VMEM((rows * row_count, cols * lanes), jnp.bfloat16)] * 2,
        compiler_params=params,
    )(recv)
    sums = lax.all_to_all(tri.reshape(world, tall, lanes), WORLD, 0, 0, tiled=True)
    weight_out = proj_out.T
    out = pl.pallas_call(
        update_kernel,
        name="update",
        grid=(tall // STEP,),
        out_shape=jax.ShapeDtypeStruct((chans, tall, lanes), jnp.bfloat16),
        in_specs=[
            pl.BlockSpec((hids, STEP, lanes), lambda i: (0, i, 0)),
            pl.BlockSpec((STEP, chans, lanes), lambda i: (i, 0, 0)),
            whole((hids, lanes)),
            whole((hids, lanes)),
            whole(weight_out.shape),
        ],
        out_specs=pl.BlockSpec((chans, STEP, lanes), lambda i: (0, i, 0)),
        scratch_shapes=[
            pltpu.VMEM((hids * STEP, lanes), jnp.float32),
            pltpu.VMEM((chans * STEP, lanes), jnp.float32),
        ],
        compiler_params=params,
    )(sums, gate, wide(gain_out), wide(bias_out), weight_out)
    return lax.all_to_all(out, "ch", 0, 1, tiled=True)


def solution(mesh):
    in_specs = (P("ch", "row", "col"),) + (P(),) * 9
    return jax.shard_map(local, mesh=mesh, in_specs=in_specs, out_specs=P("ch", "row", "col"), check_vma=False)
```

time: 723 us -> 189 us (0.26)
  waiting for transfers between devices: 465 us -> 53 us
  matrix products: 64.9 us -> 0 us
  blocking collectives: 124 us -> 92.1 us
  local copies, waits for them, and re-layouts: 31.9 us -> 7.33 us
  Pallas kernels: 0 us -> 21.7 us
  other arithmetic: 15.8 us -> 1.62 us
  between operations: 13.5 us -> 0.11 us
  starting transfers between devices: 0.37 us -> 12.4 us
    all_gather x3 -> x0, waiting for transfers between devices: 282 us -> none  [the longest x1 115 us: local(): lax.all_gather(left_act, 'col', axis=2, tiled=True)]
    reduce_scatter x1 -> x0, waiting for transfers between devices: 147 us -> none  [local(): lax.psum_scatter(partial_out, 'ch', scatter_dimension=0, tiled=True)]
    dot_general x5 -> x0, matrix products: 64.9 us -> none  [the longest x1 21.5 us: local(): jnp.einsum('hik,hjk->hij', lax.all_gather(left_act, 'col', axis=2, tiled=...]
    all_to_all x0 -> x2, waiting for transfers between devices: none -> 53 us  [the longest x1 30.2 us: local(): lax.all_to_all(tri.reshape(world, tall, lanes), WORLD, 0, 0, tiled=True)]
    psum x1 -> x0, waiting for transfers between devices: 34.7 us -> none  [local(): first_all, square_all = lax.psum((first_sum, square_sum), 'ch')]
    all_to_all x1 -> x2, blocking collectives: 124 us -> 92.1 us  [the longest x1 63.8 us: local(): lax.all_to_all(hid, WORLD, 0, 0, tiled=True)]
    all_to_all x2, local copies, waits for them, and re-layouts: 25.5 us -> 2.3 us  [the longest x1 1.49 us: local(): return lax.all_to_all(out, 'ch', 0, 1, tiled=True)]
    pallas_call x0 -> x3, Pallas kernels: none -> 21.7 us  [the longest x1 9.58 us: local(): pl.pallas_call(hidden_kernel, name='hidden', grid=(tall // STEP,), out_sh...]
  transfers between devices with their start and end apart: 5 -> 2, of which waited for: 5 -> 2; matrix products, arithmetic and copies ran while one was open for 2% -> 1% of each run, Pallas kernels for 0% -> 0%
where the time goes in v1:
time: 189 us; the launch traced here: 188 us
  blocking collectives  92.1 us (49%)
  waiting for transfers between devices  53 us (28%)
  Pallas kernels  21.7 us (11%)
  starting transfers between devices  12.4 us (7%)
  local copies, waits for them, and re-layouts  7.33 us (4%)
    all_to_all x1, blocking collectives, local(): lax.all_to_all(hid, WORLD, 0, 0, tiled=True)  63.8 us
    all_to_all x1, waiting for transfers between devices, local(): lax.all_to_all(tri.reshape(world, tall, lanes), WORLD, 0, 0, tiled=True)  30.2 us
    all_to_all x1, blocking collectives, local(): return lax.all_to_all(out, 'ch', 0, 1, tiled=True)  28.3 us
    all_to_all x1, waiting for transfers between devices, local(): mine = lax.all_to_all(pair, 'ch', 1, 0, tiled=True)  22.8 us
    pallas_call x1, Pallas kernels, local(): pl.pallas_call(hidden_kernel, name='hidden', grid=(tall // STEP,), out_sh...  9.58 us
    all_to_all x1, starting transfers between devices, local(): lax.all_to_all(tri.reshape(world, tall, lanes), WORLD, 0, 0, tiled=True)  7.26 us
    pallas_call x1, Pallas kernels, local(): pl.pallas_call(update_kernel, name='update', grid=(tall // STEP,), out_sh...  6.16 us
    pallas_call x1, Pallas kernels, local(): pl.pallas_call(triangle_kernel, name='triangle', out_shape=jax.ShapeDtype...  6 us
  transfers between devices with their start and end apart: 2, of which 2 were waited for; matrix products, arithmetic and copies ran while one was open for 1% of the time, Pallas kernels for 0%

profile of v1, /device:TPU:1, one launch (start us, length us, event | category | flops | bytes accessed | tf_op | source)
XLA Modules:
  0.0 188.3 jit_solution(4517662951576377878)
XLA Ops:
  0.0 4.3 %copy.17 = bf16[32,256,128]{2,0,1:T(8,128)(2,1)} copy(bf16[32,256,128]{2,1,0:T(8,128)(2,1)} %param.10) | data formatting | bytes 4194304 | tf_op args[0]
  4.3 0.0 copy-start
  4.3 0.0 copy-start.1
  4.3 0.0 copy-start.2
  4.3 5.1 %all-to-all-start = ((bf16[32,256,128]{2,0,1:T(8,128)(2,1)}), bf16[32,256,128]{2,0,1:T(8,128)(2,1)S(1)}, u32[]{:S(2)}, u32[]{:S(2)}) async-start(bf16[32,256,128]{2,0,1:T(8,128)(2,1)} %copy.17), calls=%async_computation | async-start | bytes 4194304 | tf_op jit(solution)/shard_map/all_to_all | solution.py:99
  9.4 0.0 copy-done
  9.4 0.1 copy.19
  9.5 0.0 copy-done.1
  9.5 0.1 copy.20
  9.6 0.0 copy-done.2
  9.7 0.1 copy.21
  9.8 0.8 dynamic-slice_convert_fusion.1
  10.5 0.8 dynamic-slice_convert_fusion
  11.3 0.1 broadcast_multiply_fusion.mask_ref
  11.4 22.8 %all-to-all-done = bf16[32,256,128]{2,0,1:T(8,128)(2,1)S(1)} async-done(((bf16[32,256,128]{2,0,1:T(8,128)(2,1)}), bf16[32,256,128]{2,0,1:T(8,128)(2,1)S(1)}, u32[]{:S(2)}, u32[]{:S(2)}) %all-to-all-start) | async-done | bytes 2097184 | tf_op jit(solution)/shard_map/all_to_all | solution.py:99
  34.2 0.0 copy-start.4
  34.2 0.0 copy-start.5
  34.2 0.8 copy.18
  35.1 0.0 copy-done.4
  35.1 0.1 broadcast_in_dim.8.gain_ref
  35.1 0.0 copy-done.5
  35.1 0.1 broadcast_in_dim.9.bias_ref
  35.2 9.6 %hidden.1 = (bf16[128,2,64,128]{3,2,1,0:T(8,128)(2,1)}, f32[64,128,128]{2,1,0:T(8,128)}) custom-call(bf16[128,64,128]{2,1,0:T(8,128)(2,1)S(1)} %bitcast.13, f32[64,128]{1,0:T(8,128)S(1)} %broadcast_multiply_fusion.mask_ref, f32[128,128]{1,0:T(8,128)S(1)} %broadcast_in_dim.8.gain_ref, f32[128,128]{1,0:T(8,128)S(1)} %broadcast_in_dim.9.bias_ref, ...), custom_call_target="tpu_custom_call" | custom-call | tf_op jit(solution)/shard_map/hidden/pallas_call | solution.py:100
  44.8 63.8 %all_to_all.46 = bf16[128,2,64,128]{3,2,1,0:T(8,128)(2,1)} all-to-all(bf16[128,2,64,128]{3,2,1,0:T(8,128)(2,1)} %get-tuple-element.7), channel_id=1, replica_groups=mesh['row'=4,'col'=8,'ch'=4] {'row','col','ch'}, dimensions={0} | all-to-all | bytes 8388608 | tf_op jit(solution)/shard_map/all_to_all | solution.py:125
  108.6 6.0 %triangle.1 = bf16[4,8,4,64,128]{4,3,2,1,0:T(8,128)(2,1)} custom-call(bf16[4,8,4,2,64,128]{5,4,3,2,1,0:T(8,128)(2,1)} %bitcast.15), custom_call_target="tpu_custom_call" | custom-call | tf_op jit(solution)/shard_map/triangle/pallas_call | solution.py:126
  114.6 0.0 copy-start.3
  114.6 0.0 copy-start.6
  114.6 0.0 copy-start.7
  114.6 7.3 %all-to-all-start.2 = ((bf16[128,64,128]{2,1,0:T(8,128)(2,1)}), bf16[128,64,128]{2,1,0:T(8,128)(2,1)S(1)}, u32[]{:S(2)}, u32[]{:S(2)}) async-start(bf16[128,64,128]{2,1,0:T(8,128)(2,1)} %bitcast.5), calls=%async_computation.2 | async-start | bytes 4194304 | tf_op jit(solution)/shard_map/all_to_all | solution.py:133
  121.9 0.0 copy-done.3
  121.9 0.1 copy.22
  122.0 30.2 %all-to-all-done.2.tri_ref = bf16[128,64,128]{2,1,0:T(8,128)(2,1)S(1)} async-done(((bf16[128,64,128]{2,1,0:T(8,128)(2,1)}), bf16[128,64,128]{2,1,0:T(8,128)(2,1)S(1)}, u32[]{:S(2)}, u32[]{:S(2)}) %all-to-all-start.2) | async-done | bytes 2097184 | tf_op jit(solution)/shard_map/all_to_all | solution.py:133
  152.1 0.0 copy-done.6
  152.2 0.1 broadcast_in_dim.10.gain_ref
  152.2 0.0 copy-done.7
  152.2 0.1 broadcast_in_dim.11.bias_ref
  152.3 6.2 %update.1 = bf16[128,64,128]{2,1,0:T(8,128)(2,1)S(1)} custom-call(bf16[128,64,128]{2,1,0:T(8,128)(2,1)S(1)} %all-to-all-done.2.tri_ref, f32[64,128,128]{2,1,0:T(8,128)} %get-tuple-element.8.gate_ref, f32[128,128]{1,0:T(8,128)S(1)} %broadcast_in_dim.10.gain_ref, f32[128,128]{1,0:T(8,128)S(1)} %broadcast_in_dim.11.bias_ref, bf16[128,128]{1,0:T(8,128)(2,1)S(1)} %bitcast.14), custom_call_target="tpu_custom_call" | custom-call | tf_op jit(solution)/shard_map/update/pallas_call | solution.py:135
  158.5 28.3 %all_to_all.47 = bf16[128,64,128]{2,1,0:T(8,128)(2,1)S(1)} all-to-all(bf16[128,64,128]{2,1,0:T(8,128)(2,1)S(1)} %update.1), channel_id=1, replica_groups=mesh['row'=4,'col'=8,'ch'=4] {'ch'}, dimensions={0} | all-to-all | bytes 4194304 | tf_op jit(solution)/shard_map/all_to_all | solution.py:154
  186.8 1.5 copy.23
  (1 shorter events, 0.0 us)
Async XLA Ops:
  4.3 5.1 %copy-start = (bf16[128,256]{1,0:T(8,128)(2,1)S(1)}, bf16[128,256]{1,0:T(8,128)(2,1)}, u32[]{:S(2)}) copy-start(bf16[128,256]{1,0:T(8,128)(2,1)} %param.15) | copy-start | bytes 196612
  4.3 5.3 %copy-start.1 = (bf16[128,256]{1,0:T(8,128)(2,1)S(1)}, bf16[128,256]{1,0:T(8,128)(2,1)}, u32[]{:S(2)}) copy-start(bf16[128,256]{1,0:T(8,128)(2,1)} %param.14) | copy-start | bytes 196612
  4.3 5.4 %copy-start.2 = (bf16[128,128]{1,0:T(8,128)(2,1)S(1)}, bf16[128,128]{1,0:T(8,128)(2,1)}, u32[]{:S(2)}) copy-start(bf16[128,128]{1,0:T(8,128)(2,1)} %param.19) | copy-start | bytes 98308
  4.3 30.0 %all-to-all-start = ((bf16[32,256,128]{2,0,1:T(8,128)(2,1)}), bf16[32,256,128]{2,0,1:T(8,128)(2,1)S(1)}, u32[]{:S(2)}, u32[]{:S(2)}) async-start(bf16[32,256,128]{2,0,1:T(8,128)(2,1)} %copy.17), calls=%async_computation | async-start | bytes 4194304 | tf_op jit(solution)/shard_map/all_to_all | solution.py:99
  34.2 0.8 copy-start.4
  34.2 0.9 copy-start.5
  114.6 7.3 %copy-start.3 = (bf16[128,128]{1,0:T(8,128)(2,1)S(1)}, bf16[128,128]{1,0:T(8,128)(2,1)}, u32[]{:S(2)}) copy-start(bf16[128,128]{1,0:T(8,128)(2,1)} %param.18) | copy-start | bytes 98308
  114.6 37.6 %copy-start.6 = (f32[128]{0:T(128)S(1)}, f32[128]{0:T(128)}, u32[]{:S(2)}) copy-start(f32[128]{0:T(128)} %param.16) | copy-start | bytes 1540
  114.6 37.6 %copy-start.7 = (f32[128]{0:T(128)S(1)}, f32[128]{0:T(128)}, u32[]{:S(2)}) copy-start(f32[128]{0:T(128)} %param.17) | copy-start | bytes 1540
  114.6 37.6 %all-to-all-start.2 = ((bf16[128,64,128]{2,1,0:T(8,128)(2,1)}), bf16[128,64,128]{2,1,0:T(8,128)(2,1)S(1)}, u32[]{:S(2)}, u32[]{:S(2)}) async-start(bf16[128,64,128]{2,1,0:T(8,128)(2,1)} %bitcast.5), calls=%async_computation.2 | async-start | bytes 4194304 | tf_op jit(solution)/shard_map/all_to_all | solution.py:133

commit v2 on v0

v2 whole, which is shorter than its diff:
```python
import functools

import jax
import jax.numpy as jnp
from jax import lax
from jax.experimental import pallas as pl
from jax.experimental.pallas import tpu as pltpu
from jax.sharding import PartitionSpec as P

epsilon = 1e-05
MESH = pl.DeviceIdType.MESH
STEP = 16
PARTS = 4
ROUNDS = 2
PER = PARTS // ROUNDS
LANES = 128
PEERS = 64


def norm_rows(values, gain, bias):
    width = values.shape[0]
    center = jnp.sum(values, axis=0, keepdims=True) * (1.0 / width)
    second = jnp.sum(values * values, axis=0, keepdims=True) * (1.0 / width)
    spread = second - center * center
    return ((values - center) * lax.rsqrt(spread + epsilon) * gain + bias).astype(jnp.bfloat16)


def sigmoid(values):
    return 0.5 * jnp.tanh(0.5 * values) + 0.5


def part_rows(r):
    return pl.ds(pl.multiple_of(r * STEP, STEP), STEP)


def kernel(
    pair_ref,
    mask_ref,
    gain_in_ref,
    bias_in_ref,
    weight_in_ref,
    gain_out_ref,
    bias_out_ref,
    weight_out_ref,
    out_ref,
    pairs,
    hidden,
    gates,
    acts,
    far,
    tri,
    sums,
    result,
    flat,
    stage,
    send_sem,
    pair_sem,
    act_sem,
    far_sem,
    sum_sem,
    out_sem,
    own_pair_sem,
    own_act_sem,
    own_sum_sem,
    own_out_sem,
):
    y, col, ch = lax.axis_index("row"), lax.axis_index("col"), lax.axis_index("ch")
    b, z = lax.div(col, 4), lax.rem(col, 4)
    low, core = lax.div(ch, 2), lax.rem(ch, 2)
    half = lax.rem(low + b, 2)
    quarter = half * 2 + core
    chan_part = pair_ref.shape[0]
    tall = STEP * PARTS

    def place(b2, y2, z2, core2):
        return {"row": y2, "col": b2 * 4 + z2, "ch": lax.rem(half + b2, 2) * 2 + core2}

    def group(b2, y2, z2, core2):
        return ((b2 * 4 + y2) * 4 + z2) * 2 + core2

    def peer(t):
        k = lax.rem(t * 37, PEERS)
        return (
            lax.rem(b + lax.div(k, 32), 2),
            lax.rem(y + lax.rem(lax.div(k, 8), 4), 4),
            lax.rem(z + lax.rem(lax.div(k, 2), 4), 4),
            lax.rem(core + lax.rem(k, 2), 2),
        )

    def across(core2):
        return {"row": y, "col": col, "ch": (1 - low) * 2 + core2}

    mine = group(b, y, z, core)
    spot = y * 2 + core

    barrier = pltpu.get_barrier_semaphore()

    def greet(t, carry):
        pl.semaphore_signal(barrier, inc=1, device_id=place(*peer(t)), device_id_type=MESH)
        return carry

    for core2 in range(2):
        pl.semaphore_signal(barrier, inc=1, device_id=across(core2), device_id_type=MESH)
    lax.fori_loop(1, PEERS, greet, 0)
    pl.semaphore_wait(barrier, PEERS + 1)

    def send_pairs(r, carry):
        for step in range(1, 4):
            ch2 = lax.rem(ch + step, 4)
            quarter2 = lax.rem(lax.div(ch2, 2) + b, 2) * 2 + lax.rem(ch2, 2)
            rows = pl.ds(pl.multiple_of(quarter2 * tall + r * STEP, STEP), STEP)
            pltpu.make_async_remote_copy(
                src_ref=pair_ref.at[:, rows, :],
                dst_ref=pairs.at[pl.ds(ch * chan_part, chan_part), part_rows(r), :],
                send_sem=send_sem.at[0],
                recv_sem=pair_sem.at[r],
                device_id={"row": y, "col": col, "ch": ch2},
                device_id_type=MESH,
            ).start()
        rows = pl.ds(pl.multiple_of(quarter * tall + r * STEP, STEP), STEP)
        pltpu.make_async_copy(
            pair_ref.at[:, rows, :],
            pairs.at[pl.ds(ch * chan_part, chan_part), part_rows(r), :],
            own_pair_sem.at[r],
        ).start()
        return carry

    lax.fori_loop(0, PARTS, send_pairs, 0)

    chans = pairs.shape[0]
    hids = hidden.shape[0]

    def make_hidden(r, carry):
        held = pairs.at[pl.ds(0, 3 * chan_part), pl.ds(0, STEP), :]
        pltpu.make_async_copy(held, held, pair_sem.at[r]).wait()
        held = pairs.at[pl.ds(0, chan_part), pl.ds(0, STEP), :]
        pltpu.make_async_copy(held, held, own_pair_sem.at[r]).wait()
        flat[...] = pairs[:, part_rows(r), :].astype(jnp.float32).reshape(chans * STEP, LANES)
        mask = mask_ref[part_rows(r), :]
        for i in range(0, STEP, 2):
            both = [
                norm_rows(flat[pl.ds(i + d, chans, stride=STEP), :], gain_in_ref[...], bias_in_ref[...])
                for d in range(2)
            ]
            prod = jnp.dot(
                weight_in_ref[...], jnp.concatenate(both, axis=1), preferred_element_type=jnp.float32
            )
            for d in range(2):
                part = prod[:, d * LANES : (d + 1) * LANES]
                act = sigmoid(part[: 2 * hids]) * part[2 * hids : 4 * hids] * mask[i + d : i + d + 1, :]
                stage[pl.ds(i + d, 2 * hids, stride=STEP), :] = act
                gates[r * STEP + (i + d)] = sigmoid(part[4 * hids :])
        rounded = stage[...].astype(jnp.bfloat16).reshape(2, hids, STEP, LANES)
        hidden[:, 0, part_rows(r), :] = rounded[0]
        hidden[:, 1, part_rows(r), :] = rounded[1]
        here = pl.ds(pl.multiple_of(r * (8 * STEP) + spot * STEP, STEP), STEP)

        def send_acts(t, inner):
            to = peer(t)
            pltpu.make_async_remote_copy(
                src_ref=hidden.at[pl.ds(2 * group(*to), 2), :, part_rows(r), :],
                dst_ref=acts.at[:, :, col, here, :],
                send_sem=send_sem.at[1],
                recv_sem=act_sem.at[r],
                device_id=place(*to),
                device_id_type=MESH,
            ).start()
            return inner

        lax.fori_loop(1, PEERS, send_acts, 0)
        pltpu.make_async_copy(
            hidden.at[pl.ds(2 * mine, 2), :, part_rows(r), :], acts.at[:, :, col, here, :], own_act_sem.at[r]
        ).start()
        return carry

    lax.fori_loop(0, PARTS, make_hidden, 0)

    def pass_right(r, carry):
        held = hidden.at[pl.ds(0, 2 * PEERS - 2), :, pl.ds(0, STEP), :]
        pltpu.make_async_copy(held, held, act_sem.at[r]).wait()
        held = hidden.at[pl.ds(0, 2), :, pl.ds(0, STEP), :]
        pltpu.make_async_copy(held, held, own_act_sem.at[r]).wait()
        rows = pl.ds(pl.multiple_of(r * (8 * STEP), 8 * STEP), 8 * STEP)
        pltpu.make_async_remote_copy(
            src_ref=acts.at[:, 1, :, rows, :],
            dst_ref=far.at[:, :, rows, :],
            send_sem=send_sem.at[2],
            recv_sem=far_sem,
            device_id=across(core),
            device_id_type=MESH,
        ).start()
        return carry

    lax.fori_loop(0, PARTS, pass_right, 0)

    def multiply(turn, load_right):
        which = lax.rem(half + turn, 2)

        def block(n, carry):
            h, m = lax.div(n, 2), lax.rem(n, 2)
            left = jnp.concatenate([acts[h, 0, c] for c in range(8)], axis=1)
            right = []
            for c in range(8):
                right.append(
                    jnp.concatenate(
                        [
                            load_right(h, c, pl.ds(pl.multiple_of(m * (4 * STEP) + (r * 8 + s) * STEP, STEP), STEP))
                            for s2 in range(2)
                            for s in (s2 * 2, s2 * 2 + 1)
                            for r in range(PARTS)
                        ],
                        axis=0,
                    )
                )
            prod = lax.dot_general(
                left,
                jnp.concatenate(right, axis=1),
                (((1,), (1,)), ((), ())),
                preferred_element_type=jnp.float32,
            ).astype(jnp.bfloat16)
            for s in range(2):
                tri[h, (m * 2 + s) * 2 + which] = prod[:, s * LANES : (s + 1) * LANES].reshape(
                    PARTS, 8 * STEP, LANES
                )
            return carry

        lax.fori_loop(0, 4, block, 0)

        def send_round(n, carry):
            part = pl.ds(n * PER, PER)

            def send_sums(t, inner):
                k = lax.rem(t * 13, PEERS // 2)
                b2 = lax.rem(b + lax.div(k, 16), 2)
                y2 = lax.rem(y + lax.rem(lax.div(k, 4), 4), 4)
                z2 = 2 * lax.rem(lax.div(z, 2) + lax.rem(lax.div(k, 2), 2), 2) + which
                core2 = lax.rem(core + lax.rem(k, 2), 2)
                src = tri.at[
                    :, b2 * 4 + z2, part, pl.ds(pl.multiple_of((y2 * 2 + core2) * STEP, STEP), STEP), :
                ]
                dst = sums.at[pl.ds(2 * mine, 2), part]
                self = jnp.logical_and(t == 0, lax.rem(z, 2) == which)

                @pl.when(self)
                def _():
                    pltpu.make_async_copy(src, dst, own_sum_sem.at[n]).start()

                @pl.when(jnp.logical_not(self))
                def _():
                    pltpu.make_async_remote_copy(
                        src_ref=src,
                        dst_ref=dst,
                        send_sem=send_sem.at[3],
                        recv_sem=sum_sem.at[n],
                        device_id=place(b2, y2, z2, core2),
                        device_id_type=MESH,
                    ).start()

                return inner

            lax.fori_loop(0, PEERS // 2, send_sums, 0)
            return carry

        lax.fori_loop(0, ROUNDS, send_round, 0)

    multiply(0, lambda h, c, rows: acts[h, 1, c, rows, :])
    pltpu.make_async_copy(far, far, far_sem).wait()
    multiply(1, lambda h, c, rows: far[h, c, rows, :])

    def make_update(r, carry):
        flat[...] = sums[:, r].astype(jnp.float32).reshape(hids * STEP, LANES)
        for i in range(0, STEP, 2):
            both = [
                norm_rows(flat[pl.ds(i + d, hids, stride=STEP), :], gain_out_ref[...], bias_out_ref[...])
                for d in range(2)
            ]
            prod = jnp.dot(
                weight_out_ref[...], jnp.concatenate(both, axis=1), preferred_element_type=jnp.float32
            )
            for d in range(2):
                stage[pl.ds(i + d, chans, stride=STEP), :] = (
                    gates[r * STEP + (i + d)] * prod[:, d * LANES : (d + 1) * LANES]
                )
        result[:, part_rows(r), :] = (
            stage[pl.ds(0, chans * STEP), :].astype(jnp.bfloat16).reshape(chans, STEP, LANES)
        )
        rows = pl.ds(pl.multiple_of(quarter * tall + r * STEP, STEP), STEP)
        for step in range(1, 4):
            ch2 = lax.rem(ch + step, 4)
            pltpu.make_async_remote_copy(
                src_ref=result.at[pl.ds(ch2 * chan_part, chan_part), part_rows(r), :],
                dst_ref=out_ref.at[:, rows, :],
                send_sem=send_sem.at[4],
                recv_sem=out_sem,
                device_id={"row": y, "col": col, "ch": ch2},
                device_id_type=MESH,
            ).start()
        pltpu.make_async_copy(
            result.at[pl.ds(ch * chan_part, chan_part), part_rows(r), :], out_ref.at[:, rows, :], own_out_sem
        ).start()
        return carry

    def take_round(n, carry):
        held = sums.at[pl.ds(0, 2 * PEERS - 2), pl.ds(0, PER)]
        pltpu.make_async_copy(held, held, sum_sem.at[n]).wait()
        held = sums.at[pl.ds(0, 2), pl.ds(0, PER)]
        pltpu.make_async_copy(held, held, own_sum_sem.at[n]).wait()
        lax.fori_loop(n * PER, n * PER + PER, make_update, 0)
        return carry

    lax.fori_loop(0, ROUNDS, take_round, 0)

    held = result.at[pl.ds(0, 3 * chan_part)]
    pltpu.make_async_copy(held, held, out_sem).wait()
    held = result.at[pl.ds(0, chan_part)]
    pltpu.make_async_copy(held, held, own_out_sem).wait()
    for n, held in enumerate(
        (
            pairs.at[pl.ds(0, 3 * chan_part)],
            hidden.at[pl.ds(0, 2 * PEERS - 2)],
            far,
            sums.at[pl.ds(0, 2 * PEERS - 2)],
            result.at[pl.ds(0, 3 * chan_part)],
        )
    ):
        pltpu.make_async_copy(held, held, send_sem.at[n]).wait()


def local(pair, token_mask, gain_in, bias_in, proj_in, gate_in, gain_out, bias_out, proj_out, gate_out):
    chan_part, row_count, lanes = pair.shape
    chs = lax.axis_size("ch")
    chans, hids = chan_part * chs, proj_out.shape[0]
    tall = row_count // chs
    ch, col = lax.axis_index("ch"), lax.axis_index("col")
    quarter = (ch // 2 + col // 4) % 2 * 2 + ch % 2
    row_start = lax.axis_index("row") * row_count + quarter * tall
    row_mask = lax.dynamic_slice_in_dim(token_mask, row_start, tall, 0).astype(jnp.float32)
    col_mask = lax.dynamic_slice_in_dim(token_mask, col * lanes, lanes, 0).astype(jnp.float32)
    mask = row_mask[:, None] * col_mask[None, :]
    wide = lambda v: jnp.broadcast_to(v[:, None], (v.shape[0], lanes))
    weight = jnp.concatenate([gate_in, proj_in, gate_out], axis=1).T
    vmem = pl.BlockSpec(memory_space=pltpu.VMEM)
    half16 = lambda *shape: pltpu.VMEM(shape, jnp.bfloat16)
    dma = pltpu.SemaphoreType.DMA
    return pl.pallas_call(
        kernel,
        name="update",
        out_shape=jax.ShapeDtypeStruct(pair.shape, jnp.bfloat16),
        in_specs=[pl.BlockSpec(memory_space=pl.ANY)] + [vmem] * 7,
        out_specs=pl.BlockSpec(memory_space=pl.ANY),
        scratch_shapes=[
            half16(chans, tall, lanes),
            half16(hids, 2, tall, lanes),
            pltpu.VMEM((tall, chans, lanes), jnp.float32),
            half16(2, 2, 8, PARTS * 8 * STEP, lanes),
            half16(2, 8, PARTS * 8 * STEP, lanes),
            half16(2, 8, PARTS, 8 * STEP, lanes),
            half16(hids, PARTS, STEP, lanes),
            half16(chans, tall, lanes),
            pltpu.VMEM((chans * STEP, lanes), jnp.float32),
            pltpu.VMEM((2 * hids * STEP, lanes), jnp.float32),
            dma((5,)),
            dma((PARTS,)),
            dma((PARTS,)),
            dma,
            dma((ROUNDS,)),
            dma,
            dma((PARTS,)),
            dma((PARTS,)),
            dma((ROUNDS,)),
            dma,
        ],
        compiler_params=pltpu.CompilerParams(
            collective_id=0, has_side_effects=True, vmem_limit_bytes=56 * 2**20
        ),
    )(pair, mask, wide(gain_in), wide(bias_in), weight, wide(gain_out), wide(bias_out), proj_out.T)


def solution(mesh):
    in_specs = (P("ch", "row", "col"),) + (P(),) * 9
    return jax.shard_map(local, mesh=mesh, in_specs=in_specs, out_specs=P("ch", "row", "col"), check_vma=False)
```

time: 723 us -> 154 us (0.21)
  waiting for transfers between devices: 465 us -> 0 us
  Pallas kernels: 0 us -> 137 us
  blocking collectives: 124 us -> 0 us
  matrix products: 64.9 us -> 0 us
  local copies, waits for them, and re-layouts: 31.9 us -> 12.8 us
  between operations: 13.5 us -> 0.03 us
  other arithmetic: 15.8 us -> 2.88 us
    all_gather x3 -> x0, waiting for transfers between devices: 282 us -> none  [the longest x1 115 us: local(): lax.all_gather(left_act, 'col', axis=2, tiled=True)]
    reduce_scatter x1 -> x0, waiting for transfers between devices: 147 us -> none  [local(): lax.psum_scatter(partial_out, 'ch', scatter_dimension=0, tiled=True)]
    pallas_call x0 -> x1, Pallas kernels: none -> 137 us  [local(): pl.pallas_call(kernel, name='update', out_shape=jax.ShapeDtypeStruct(pair...]
    all_to_all x1 -> x0, blocking collectives: 124 us -> none  [local(): lax.all_to_all(right_all, 'col', split_axis=1, concat_axis=2, tiled=True)]
    dot_general x5 -> x0, matrix products: 64.9 us -> none  [the longest x1 21.5 us: local(): jnp.einsum('hik,hjk->hij', lax.all_gather(left_act, 'col', axis=2, tiled=...]
    psum x1 -> x0, waiting for transfers between devices: 34.7 us -> none  [local(): first_all, square_all = lax.psum((first_sum, square_sum), 'ch')]
    all_to_all x2 -> x0, local copies, waits for them, and re-layouts: 25.5 us -> none  [local(): lax.all_to_all(right_all, 'col', split_axis=1, concat_axis=2, tiled=True)]
    convert_element_type x4 -> x2, other arithmetic: 8.89 us -> 1.52 us  [the longest x1 0.76 us: local(): lax.dynamic_slice_in_dim(token_mask, col * lanes, lanes, 0)]
  transfers between devices with their start and end apart: 5 -> 0, of which waited for: 5 -> 0; matrix products, arithmetic and copies ran while one was open for 2% -> 0% of each run, Pallas kernels for 0% -> 0%
where the time goes in v2:
time: 154 us; the launch traced here: 153 us
  Pallas kernels  137 us (89%)
  local copies, waits for them, and re-layouts  12.8 us (8%)
  other arithmetic  2.88 us (2%)
    pallas_call x1, Pallas kernels, local(): pl.pallas_call(kernel, name='update', out_shape=jax.ShapeDtypeStruct(pair...  137 us
    unnamed x5, local copies, waits for them, and re-layouts  7.37 us
    broadcast_in_dim x4, local copies, waits for them, and re-layouts, local(): wide = lambda v: jnp.broadcast_to(v[:, None], (v.shape[0], lanes))  5.43 us

profile of v2, /device:TPU:1, one launch (start us, length us, event | category | flops | bytes accessed | tf_op | source)
XLA Modules:
  0.0 153.2 jit_solution(9574813802810461427)
XLA Ops:
  0.0 0.8 dynamic-slice_convert_fusion
  0.8 0.8 dynamic-slice_convert_fusion.1
  1.5 0.7 broadcast_multiply_fusion.mask_ref
  2.2 1.5 copy.14
  3.7 0.9 copy.13
  4.5 1.4 broadcast_in_dim.8.gain_in_ref
  5.9 1.4 broadcast_in_dim.9.bias_in_ref
  7.3 0.9 copy.12
  8.2 1.0 copy.11
  9.2 0.7 maximum_bitcast_fusion.weight_in_ref
  9.9 1.4 broadcast_in_dim.10.gain_out_ref
  11.2 1.4 broadcast_in_dim.11.bias_out_ref
  12.6 137.5 %update.1 = bf16[32,256,128]{2,1,0:T(8,128)(2,1)} custom-call(bf16[32,256,128]{2,1,0:T(8,128)(2,1)} %pair_ref.1, f32[64,128]{1,0:T(8,128)} %broadcast_multiply_fusion.mask_ref, f32[128,128]{1,0:T(8,128)} %broadcast_in_dim.8.gain_in_ref, f32[128,128]{1,0:T(8,128)} %broadcast_in_dim.9.bias_in_ref, bf16[640,128]{1,0:T(8,128)(2,1)} %maximum_bitcast_fusion.weight_in_ref, ...), custom_call_target="tpu_custom_call" | custom-call | tf_op jit(solution)/shard_map/update/pallas_call | solution.py:345
  150.0 3.1 %copy.16 = bf16[32,256,128]{2,1,0:T(8,128)(2,1)} copy(bf16[32,256,128]{2,1,0:T(8,128)(2,1)} %update.1) | data formatting | bytes 4194304

commit v3 on v2

--- a/solution.py
+++ b/solution.py
@@ -11,7 +11,7 @@
 MESH = pl.DeviceIdType.MESH
 STEP = 16
 PARTS = 4
-ROUNDS = 2
+ROUNDS = 4
 PER = PARTS // ROUNDS
 LANES = 128
 PEERS = 64
@@ -35,13 +35,15 @@
 
 def kernel(
     pair_ref,
-    mask_ref,
+    token_ref,
     gain_in_ref,
     bias_in_ref,
-    weight_in_ref,
+    proj_in_ref,
+    gate_in_ref,
     gain_out_ref,
     bias_out_ref,
-    weight_out_ref,
+    proj_out_ref,
+    gate_out_ref,
     out_ref,
     pairs,
     hidden,
@@ -53,6 +55,10 @@
     result,
     flat,
     stage,
+    mask,
+    affine,
+    weight_in,
+    weight_out,
     send_sem,
     pair_sem,
     act_sem,
@@ -130,24 +136,40 @@
     chans = pairs.shape[0]
     hids = hidden.shape[0]
 
+    def turned(ref):
+        return ref[...].astype(jnp.float32).T.astype(jnp.bfloat16)
+
+    def column(vec):
+        return jnp.broadcast_to(vec, (LANES, LANES)).T
+
+    weight_in[: 2 * hids] = turned(gate_in_ref)
+    weight_in[2 * hids : 4 * hids] = turned(proj_in_ref)
+    weight_in[4 * hids :] = turned(gate_out_ref)
+    weight_out[...] = turned(proj_out_ref)
+    for n, ref in enumerate((gain_in_ref, bias_in_ref, gain_out_ref, bias_out_ref)):
+        affine[n] = column(ref[...])
+    mask[...] = column(token_ref[pl.ds(y * 2 + half, 1), :].astype(jnp.float32)) * token_ref[
+        pl.ds(col, 1), :
+    ].astype(jnp.float32)
+
     def make_hidden(r, carry):
         held = pairs.at[pl.ds(0, 3 * chan_part), pl.ds(0, STEP), :]
         pltpu.make_async_copy(held, held, pair_sem.at[r]).wait()
         held = pairs.at[pl.ds(0, chan_part), pl.ds(0, STEP), :]
         pltpu.make_async_copy(held, held, own_pair_sem.at[r]).wait()
         flat[...] = pairs[:, part_rows(r), :].astype(jnp.float32).reshape(chans * STEP, LANES)
-        mask = mask_ref[part_rows(r), :]
+        here_mask = mask[pl.ds(pl.multiple_of(core * tall + r * STEP, STEP), STEP), :]
         for i in range(0, STEP, 2):
             both = [
-                norm_rows(flat[pl.ds(i + d, chans, stride=STEP), :], gain_in_ref[...], bias_in_ref[...])
+                norm_rows(flat[pl.ds(i + d, chans, stride=STEP), :], affine[0], affine[1])
                 for d in range(2)
             ]
             prod = jnp.dot(
-                weight_in_ref[...], jnp.concatenate(both, axis=1), preferred_element_type=jnp.float32
+                weight_in[...], jnp.concatenate(both, axis=1), preferred_element_type=jnp.float32
             )
             for d in range(2):
                 part = prod[:, d * LANES : (d + 1) * LANES]
-                act = sigmoid(part[: 2 * hids]) * part[2 * hids : 4 * hids] * mask[i + d : i + d + 1, :]
+                act = sigmoid(part[: 2 * hids]) * part[2 * hids : 4 * hids] * here_mask[i + d : i + d + 1, :]
                 stage[pl.ds(i + d, 2 * hids, stride=STEP), :] = act
                 gates[r * STEP + (i + d)] = sigmoid(part[4 * hids :])
         rounded = stage[...].astype(jnp.bfloat16).reshape(2, hids, STEP, LANES)
@@ -226,56 +248,46 @@
 
         lax.fori_loop(0, 4, block, 0)
 
-        def send_round(n, carry):
-            part = pl.ds(n * PER, PER)
-
-            def send_sums(t, inner):
-                k = lax.rem(t * 13, PEERS // 2)
-                b2 = lax.rem(b + lax.div(k, 16), 2)
-                y2 = lax.rem(y + lax.rem(lax.div(k, 4), 4), 4)
-                z2 = 2 * lax.rem(lax.div(z, 2) + lax.rem(lax.div(k, 2), 2), 2) + which
-                core2 = lax.rem(core + lax.rem(k, 2), 2)
-                src = tri.at[
-                    :, b2 * 4 + z2, part, pl.ds(pl.multiple_of((y2 * 2 + core2) * STEP, STEP), STEP), :
-                ]
-                dst = sums.at[pl.ds(2 * mine, 2), part]
-                self = jnp.logical_and(t == 0, lax.rem(z, 2) == which)
-
-                @pl.when(self)
-                def _():
-                    pltpu.make_async_copy(src, dst, own_sum_sem.at[n]).start()
-
-                @pl.when(jnp.logical_not(self))
-                def _():
-                    pltpu.make_async_remote_copy(
-                        src_ref=src,
-                        dst_ref=dst,
-                        send_sem=send_sem.at[3],
-                        recv_sem=sum_sem.at[n],
-                        device_id=place(b2, y2, z2, core2),
-                        device_id_type=MESH,
-                    ).start()
-
-                return inner
-
-            lax.fori_loop(0, PEERS // 2, send_sums, 0)
-            return carry
-
-        lax.fori_loop(0, ROUNDS, send_round, 0)
-
     multiply(0, lambda h, c, rows: acts[h, 1, c, rows, :])
     pltpu.make_async_copy(far, far, far_sem).wait()
     multiply(1, lambda h, c, rows: far[h, c, rows, :])
+
+    def send_round(n, carry):
+        part = pl.ds(n * PER, PER)
+
+        def send_sums(t, inner):
+            b2, y2, z2, core2 = peer(t)
+            pltpu.make_async_remote_copy(
+                src_ref=tri.at[
+                    :, b2 * 4 + z2, part, pl.ds(pl.multiple_of((y2 * 2 + core2) * STEP, STEP), STEP), :
+                ],
+                dst_ref=sums.at[pl.ds(2 * mine, 2), part],
+                send_sem=send_sem.at[3],
+                recv_sem=sum_sem.at[n],
+                device_id=place(b2, y2, z2, core2),
+                device_id_type=MESH,
+            ).start()
+            return inner
+
+        lax.fori_loop(1, PEERS, send_sums, 0)
+        pltpu.make_async_copy(
+            tri.at[:, col, part, pl.ds(pl.multiple_of(spot * STEP, STEP), STEP), :],
+            sums.at[pl.ds(2 * mine, 2), part],
+            own_sum_sem.at[n],
+        ).start()
+        return carry
+
+    lax.fori_loop(0, ROUNDS, send_round, 0)
 
     def make_update(r, carry):
         flat[...] = sums[:, r].astype(jnp.float32).reshape(hids * STEP, LANES)
         for i in range(0, STEP, 2):
             both = [
-                norm_rows(flat[pl.ds(i + d, hids, stride=STEP), :], gain_out_ref[...], bias_out_ref[...])
+                norm_rows(flat[pl.ds(i + d, hids, stride=STEP), :], affine[2], affine[3])
                 for d in range(2)
             ]
             prod = jnp.dot(
-                weight_out_ref[...], jnp.concatenate(both, axis=1), preferred_element_type=jnp.float32
+                weight_out[...], jnp.concatenate(both, axis=1), preferred_element_type=jnp.float32
             )
             for d in range(2):
                 stage[pl.ds(i + d, chans, stride=STEP), :] = (
@@ -331,14 +343,6 @@
     chs = lax.axis_size("ch")
     chans, hids = chan_part * chs, proj_out.shape[0]
     tall = row_count // chs
-    ch, col = lax.axis_index("ch"), lax.axis_index("col")
-    quarter = (ch // 2 + col // 4) % 2 * 2 + ch % 2
-    row_start = lax.axis_index("row") * row_count + quarter * tall
-    row_mask = lax.dynamic_slice_in_dim(token_mask, row_start, tall, 0).astype(jnp.float32)
-    col_mask = lax.dynamic_slice_in_dim(token_mask, col * lanes, lanes, 0).astype(jnp.float32)
-    mask = row_mask[:, None] * col_mask[None, :]
-    wide = lambda v: jnp.broadcast_to(v[:, None], (v.shape[0], lanes))
-    weight = jnp.concatenate([gate_in, proj_in, gate_out], axis=1).T
     vmem = pl.BlockSpec(memory_space=pltpu.VMEM)
     half16 = lambda *shape: pltpu.VMEM(shape, jnp.bfloat16)
     dma = pltpu.SemaphoreType.DMA
@@ -346,7 +350,7 @@
         kernel,
         name="update",
         out_shape=jax.ShapeDtypeStruct(pair.shape, jnp.bfloat16),
-        in_specs=[pl.BlockSpec(memory_space=pl.ANY)] + [vmem] * 7,
+        in_specs=[pl.BlockSpec(memory_space=pl.ANY)] + [vmem] * 9,
         out_specs=pl.BlockSpec(memory_space=pl.ANY),
         scratch_shapes=[
             half16(chans, tall, lanes),
@@ -359,6 +363,10 @@
             half16(chans, tall, lanes),
             pltpu.VMEM((chans * STEP, lanes), jnp.float32),
             pltpu.VMEM((2 * hids * STEP, lanes), jnp.float32),
+            pltpu.VMEM((lanes, lanes), jnp.float32),
+            pltpu.VMEM((4, lanes, lanes), jnp.float32),
+            half16(4 * hids + chans, chans),
+            half16(chans, hids),
             dma((5,)),
             dma((PARTS,)),
             dma((PARTS,)),
@@ -373,7 +381,18 @@
         compiler_params=pltpu.CompilerParams(
             collective_id=0, has_side_effects=True, vmem_limit_bytes=56 * 2**20
         ),
-    )(pair, mask, wide(gain_in), wide(bias_in), weight, wide(gain_out), wide(bias_out), proj_out.T)
+    )(
+        pair,
+        token_mask.reshape(-1, lanes),
+        gain_in.reshape(1, -1),
+        bias_in.reshape(1, -1),
+        proj_in,
+        gate_in,
+        gain_out.reshape(1, -1),
+        bias_out.reshape(1, -1),
+        proj_out,
+        gate_out,
+    )
 
 
 def solution(mesh):

time: 154 us -> 126 us (0.82)
  Pallas kernels: 137 us -> 123 us
  local copies, waits for them, and re-layouts: 12.8 us -> 3.14 us
  other arithmetic: 2.88 us -> 0 us
    pallas_call x1, Pallas kernels: 137 us -> 123 us  [local(): pl.pallas_call(kernel, name='update', out_shape=jax.ShapeDtypeStruct(pair...]
    broadcast_in_dim x4 -> x0, local copies, waits for them, and re-layouts: 5.43 us -> none  [local(): wide = lambda v: jnp.broadcast_to(v[:, None], (v.shape[0], lanes))]
    unnamed x5 -> x1, local copies, waits for them, and re-layouts: 7.37 us -> 3.14 us
where the time goes in v3:
time: 126 us
  Pallas kernels  123 us (98%)
  local copies, waits for them, and re-layouts  3.14 us (2%)
    pallas_call x1, Pallas kernels, local(): pl.pallas_call(kernel, name='update', out_shape=jax.ShapeDtypeStruct(pair...  123 us
    unnamed x1, local copies, waits for them, and re-layouts  3.14 us

profile of v3, /device:TPU:1, one launch (start us, length us, event | category | flops | bytes accessed | tf_op | source)
XLA Modules:
  0.0 126.2 jit_solution(13739581799698115060)
XLA Ops:
  0.0 123.1 %update.1 = bf16[32,256,128]{2,1,0:T(8,128)(2,1)} custom-call(bf16[32,256,128]{2,1,0:T(8,128)(2,1)} %pair_ref.1, s32[8,128]{1,0:T(8,128)} %bitcast.5, f32[1,128]{1,0:T(1,128)} %bitcast.6, f32[1,128]{1,0:T(1,128)} %bitcast.7, bf16[128,256]{1,0:T(8,128)(2,1)} %proj_in_ref.1, bf16[128,256]{1,0:T(8,128)(2,1)} %gate_in_ref.1, f32[1,128]{1,0:T(1,128)} %bitcast.8, ...), custom_call_target="tpu_custom_call" | custom-call | tf_op jit(solution)/shard_map/update/pallas_call | solution.py:349
  123.1 3.1 %copy.12 = bf16[32,256,128]{2,1,0:T(8,128)(2,1)} copy(bf16[32,256,128]{2,1,0:T(8,128)(2,1)} %update.1) | data formatting | bytes 4194304

commit v4 on v3

--- a/solution.py
+++ b/solution.py
@@ -14,6 +14,7 @@
 ROUNDS = 4
 PER = PARTS // ROUNDS
 LANES = 128
+SPARE = PARTS - 1
 PEERS = 64
 
 
@@ -35,15 +36,15 @@
 
 def kernel(
     pair_ref,
-    token_ref,
-    gain_in_ref,
-    bias_in_ref,
-    proj_in_ref,
-    gate_in_ref,
-    gain_out_ref,
-    bias_out_ref,
-    proj_out_ref,
-    gate_out_ref,
+    token_hbm,
+    gain_in_hbm,
+    bias_in_hbm,
+    proj_in_hbm,
+    gate_in_hbm,
+    gain_out_hbm,
+    bias_out_hbm,
+    proj_out_hbm,
+    gate_out_hbm,
     out_ref,
     pairs,
     hidden,
@@ -59,16 +60,29 @@
     affine,
     weight_in,
     weight_out,
+    extra,
+    token_ref,
+    gain_in_ref,
+    bias_in_ref,
+    proj_in_ref,
+    gate_in_ref,
+    gain_out_ref,
+    bias_out_ref,
+    proj_out_ref,
+    gate_out_ref,
     send_sem,
     pair_sem,
     act_sem,
+    extra_sem,
     far_sem,
     sum_sem,
     out_sem,
     own_pair_sem,
     own_act_sem,
+    own_extra_sem,
     own_sum_sem,
     own_out_sem,
+    small_sem,
 ):
     y, col, ch = lax.axis_index("row"), lax.axis_index("col"), lax.axis_index("ch")
     b, z = lax.div(col, 4), lax.rem(col, 4)
@@ -96,6 +110,25 @@
     def across(core2):
         return {"row": y, "col": col, "ch": (1 - low) * 2 + core2}
 
+    small = [
+        pltpu.make_async_copy(src, dst, small_sem.at[n])
+        for n, (src, dst) in enumerate(
+            (
+                (token_hbm, token_ref),
+                (gain_in_hbm, gain_in_ref),
+                (bias_in_hbm, bias_in_ref),
+                (proj_in_hbm, proj_in_ref),
+                (gate_in_hbm, gate_in_ref),
+                (gain_out_hbm, gain_out_ref),
+                (bias_out_hbm, bias_out_ref),
+                (proj_out_hbm, proj_out_ref),
+                (gate_out_hbm, gate_out_ref),
+            )
+        )
+    ]
+    for copy in small:
+        copy.start()
+
     mine = group(b, y, z, core)
     spot = y * 2 + core
 
@@ -110,28 +143,30 @@
     lax.fori_loop(1, PEERS, greet, 0)
     pl.semaphore_wait(barrier, PEERS + 1)
 
+    def rows_for(half2, core2, r):
+        spare = lax.div(r, PARTS)
+        half2 = lax.rem(half2 + spare, 2)
+        return pl.ds(pl.multiple_of((half2 * 2 + core2) * tall + (r - spare) * STEP, STEP), STEP)
+
     def send_pairs(r, carry):
         for step in range(1, 4):
             ch2 = lax.rem(ch + step, 4)
-            quarter2 = lax.rem(lax.div(ch2, 2) + b, 2) * 2 + lax.rem(ch2, 2)
-            rows = pl.ds(pl.multiple_of(quarter2 * tall + r * STEP, STEP), STEP)
             pltpu.make_async_remote_copy(
-                src_ref=pair_ref.at[:, rows, :],
+                src_ref=pair_ref.at[:, rows_for(lax.rem(lax.div(ch2, 2) + b, 2), lax.rem(ch2, 2), r), :],
                 dst_ref=pairs.at[pl.ds(ch * chan_part, chan_part), part_rows(r), :],
                 send_sem=send_sem.at[0],
                 recv_sem=pair_sem.at[r],
                 device_id={"row": y, "col": col, "ch": ch2},
                 device_id_type=MESH,
             ).start()
-        rows = pl.ds(pl.multiple_of(quarter * tall + r * STEP, STEP), STEP)
         pltpu.make_async_copy(
-            pair_ref.at[:, rows, :],
+            pair_ref.at[:, rows_for(half, core, r), :],
             pairs.at[pl.ds(ch * chan_part, chan_part), part_rows(r), :],
             own_pair_sem.at[r],
         ).start()
         return carry
 
-    lax.fori_loop(0, PARTS, send_pairs, 0)
+    lax.fori_loop(0, PARTS + 1, send_pairs, 0)
 
     chans = pairs.shape[0]
     hids = hidden.shape[0]
@@ -142,31 +177,37 @@
     def column(vec):
         return jnp.broadcast_to(vec, (LANES, LANES)).T
 
+    for copy in small:
+        copy.wait()
     weight_in[: 2 * hids] = turned(gate_in_ref)
     weight_in[2 * hids : 4 * hids] = turned(proj_in_ref)
     weight_in[4 * hids :] = turned(gate_out_ref)
     weight_out[...] = turned(proj_out_ref)
     for n, ref in enumerate((gain_in_ref, bias_in_ref, gain_out_ref, bias_out_ref)):
         affine[n] = column(ref[...])
-    mask[...] = column(token_ref[pl.ds(y * 2 + half, 1), :].astype(jnp.float32)) * token_ref[
-        pl.ds(col, 1), :
-    ].astype(jnp.float32)
-
-    def make_hidden(r, carry):
+    for n in range(2):
+        mask[n] = column(
+            token_ref[pl.ds(y * 2 + lax.rem(half + n, 2), 1), :].astype(jnp.float32)
+        ) * token_ref[pl.ds(col, 1), :].astype(jnp.float32)
+
+    def take_pairs(r):
         held = pairs.at[pl.ds(0, 3 * chan_part), pl.ds(0, STEP), :]
         pltpu.make_async_copy(held, held, pair_sem.at[r]).wait()
         held = pairs.at[pl.ds(0, chan_part), pl.ds(0, STEP), :]
         pltpu.make_async_copy(held, held, own_pair_sem.at[r]).wait()
         flat[...] = pairs[:, part_rows(r), :].astype(jnp.float32).reshape(chans * STEP, LANES)
-        here_mask = mask[pl.ds(pl.multiple_of(core * tall + r * STEP, STEP), STEP), :]
+
+    def normed(i):
+        both = [
+            norm_rows(flat[pl.ds(i + d, chans, stride=STEP), :], affine[0], affine[1]) for d in range(2)
+        ]
+        return jnp.concatenate(both, axis=1)
+
+    def make_hidden(r, carry):
+        take_pairs(r)
+        here_mask = mask[0, pl.ds(pl.multiple_of(core * tall + r * STEP, STEP), STEP), :]
         for i in range(0, STEP, 2):
-            both = [
-                norm_rows(flat[pl.ds(i + d, chans, stride=STEP), :], affine[0], affine[1])
-                for d in range(2)
-            ]
-            prod = jnp.dot(
-                weight_in[...], jnp.concatenate(both, axis=1), preferred_element_type=jnp.float32
-            )
+            prod = jnp.dot(weight_in[...], normed(i), preferred_element_type=jnp.float32)
             for d in range(2):
                 part = prod[:, d * LANES : (d + 1) * LANES]
                 act = sigmoid(part[: 2 * hids]) * part[2 * hids : 4 * hids] * here_mask[i + d : i + d + 1, :]
@@ -197,12 +238,15 @@
 
     lax.fori_loop(0, PARTS, make_hidden, 0)
 
-    def pass_right(r, carry):
+    def take_acts(r):
         held = hidden.at[pl.ds(0, 2 * PEERS - 2), :, pl.ds(0, STEP), :]
         pltpu.make_async_copy(held, held, act_sem.at[r]).wait()
         held = hidden.at[pl.ds(0, 2), :, pl.ds(0, STEP), :]
         pltpu.make_async_copy(held, held, own_act_sem.at[r]).wait()
-        rows = pl.ds(pl.multiple_of(r * (8 * STEP), 8 * STEP), 8 * STEP)
+
+    def pass_right(r):
+        take_acts(r)
+        rows = pl.ds(r * (8 * STEP), 8 * STEP)
         pltpu.make_async_remote_copy(
             src_ref=acts.at[:, 1, :, rows, :],
             dst_ref=far.at[:, :, rows, :],
@@ -211,9 +255,43 @@
             device_id=across(core),
             device_id_type=MESH,
         ).start()
-        return carry
-
-    lax.fori_loop(0, PARTS, pass_right, 0)
+
+    pass_right(0)
+
+    take_pairs(PARTS)
+    spare_mask = mask[1, pl.ds(pl.multiple_of(core * tall + SPARE * STEP, STEP), STEP), :]
+    for i in range(0, STEP, 2):
+        both = normed(i)
+        gate = jnp.dot(weight_in[hids : 2 * hids], both, preferred_element_type=jnp.float32)
+        prod = jnp.dot(weight_in[3 * hids : 4 * hids], both, preferred_element_type=jnp.float32)
+        for d in range(2):
+            lanes = slice(d * LANES, (d + 1) * LANES)
+            stage[pl.ds(i + d, hids, stride=STEP), :] = (
+                sigmoid(gate[:, lanes]) * prod[:, lanes] * spare_mask[i + d : i + d + 1, :]
+            )
+    extra[...] = stage[pl.ds(0, hids * STEP), :].astype(jnp.bfloat16).reshape(hids, STEP, LANES)
+    spare_rows = pl.ds(pl.multiple_of(SPARE * (8 * STEP) + spot * STEP, STEP), STEP)
+
+    def send_extra(t, carry):
+        to = peer(t)
+        pltpu.make_async_remote_copy(
+            src_ref=extra.at[pl.ds(2 * group(*to), 2)],
+            dst_ref=far.at[:, col, spare_rows, :],
+            send_sem=send_sem.at[5],
+            recv_sem=extra_sem,
+            device_id=place(*to),
+            device_id_type=MESH,
+        ).start()
+        return carry
+
+    lax.fori_loop(1, PEERS, send_extra, 0)
+    pltpu.make_async_copy(
+        extra.at[pl.ds(2 * mine, 2)], far.at[:, col, spare_rows, :], own_extra_sem
+    ).start()
+
+    for r in range(1, SPARE):
+        pass_right(r)
+    take_acts(SPARE)
 
     def multiply(turn, load_right):
         which = lax.rem(half + turn, 2)
@@ -249,7 +327,12 @@
         lax.fori_loop(0, 4, block, 0)
 
     multiply(0, lambda h, c, rows: acts[h, 1, c, rows, :])
-    pltpu.make_async_copy(far, far, far_sem).wait()
+    held = extra.at[pl.ds(0, 2 * PEERS - 2)]
+    pltpu.make_async_copy(held, held, extra_sem).wait()
+    held = extra.at[pl.ds(0, 2)]
+    pltpu.make_async_copy(held, held, own_extra_sem).wait()
+    held = far.at[:, :, pl.ds(0, SPARE * 8 * STEP), :]
+    pltpu.make_async_copy(held, held, far_sem).wait()
     multiply(1, lambda h, c, rows: far[h, c, rows, :])
 
     def send_round(n, carry):
@@ -330,9 +413,10 @@
         (
             pairs.at[pl.ds(0, 3 * chan_part)],
             hidden.at[pl.ds(0, 2 * PEERS - 2)],
-            far,
+            far.at[:, :, pl.ds(0, SPARE * 8 * STEP), :],
             sums.at[pl.ds(0, 2 * PEERS - 2)],
             result.at[pl.ds(0, 3 * chan_part)],
+            extra.at[pl.ds(0, 2 * PEERS - 2)],
         )
     ):
         pltpu.make_async_copy(held, held, send_sem.at[n]).wait()
@@ -343,17 +427,16 @@
     chs = lax.axis_size("ch")
     chans, hids = chan_part * chs, proj_out.shape[0]
     tall = row_count // chs
-    vmem = pl.BlockSpec(memory_space=pltpu.VMEM)
     half16 = lambda *shape: pltpu.VMEM(shape, jnp.bfloat16)
     dma = pltpu.SemaphoreType.DMA
     return pl.pallas_call(
         kernel,
         name="update",
         out_shape=jax.ShapeDtypeStruct(pair.shape, jnp.bfloat16),
-        in_specs=[pl.BlockSpec(memory_space=pl.ANY)] + [vmem] * 9,
+        in_specs=[pl.BlockSpec(memory_space=pl.ANY)] + [pl.BlockSpec(memory_space=pl.ANY)] * 9,
         out_specs=pl.BlockSpec(memory_space=pl.ANY),
         scratch_shapes=[
-            half16(chans, tall, lanes),
+            half16(chans, tall + STEP, lanes),
             half16(hids, 2, tall, lanes),
             pltpu.VMEM((tall, chans, lanes), jnp.float32),
             half16(2, 2, 8, PARTS * 8 * STEP, lanes),
@@ -363,20 +446,33 @@
             half16(chans, tall, lanes),
             pltpu.VMEM((chans * STEP, lanes), jnp.float32),
             pltpu.VMEM((2 * hids * STEP, lanes), jnp.float32),
-            pltpu.VMEM((lanes, lanes), jnp.float32),
+            pltpu.VMEM((2, lanes, lanes), jnp.float32),
             pltpu.VMEM((4, lanes, lanes), jnp.float32),
             half16(4 * hids + chans, chans),
             half16(chans, hids),
-            dma((5,)),
+            half16(hids, STEP, lanes),
+            pltpu.VMEM((token_mask.shape[0] // lanes, lanes), jnp.int32),
+            pltpu.VMEM((1, lanes), jnp.float32),
+            pltpu.VMEM((1, lanes), jnp.float32),
+            half16(*proj_in.shape),
+            half16(*gate_in.shape),
+            pltpu.VMEM((1, lanes), jnp.float32),
+            pltpu.VMEM((1, lanes), jnp.float32),
+            half16(*proj_out.shape),
+            half16(*gate_out.shape),
+            dma((6,)),
+            dma((PARTS + 1,)),
             dma((PARTS,)),
+            dma,
+            dma,
+            dma((ROUNDS,)),
+            dma,
+            dma((PARTS + 1,)),
             dma((PARTS,)),
             dma,
             dma((ROUNDS,)),
             dma,
-            dma((PARTS,)),
-            dma((PARTS,)),
-            dma((ROUNDS,)),
-            dma,
+            dma((9,)),
         ],
         compiler_params=pltpu.CompilerParams(
             collective_id=0, has_side_effects=True, vmem_limit_bytes=56 * 2**20

time: 126 us -> 116 us (0.921)
  Pallas kernels: 123 us -> 113 us
    pallas_call x1, Pallas kernels: 123 us -> 113 us  [local(): pl.pallas_call(kernel, name='update', out_shape=jax.ShapeDtypeStruct(pair...]
where the time goes in v4:
time: 116 us
  Pallas kernels  113 us (97%)
  local copies, waits for them, and re-layouts  3.14 us (3%)
    pallas_call x1, Pallas kernels, local(): pl.pallas_call(kernel, name='update', out_shape=jax.ShapeDtypeStruct(pair...  113 us
    unnamed x1, local copies, waits for them, and re-layouts  3.14 us

profile of v4, /device:TPU:1, one launch (start us, length us, event | category | flops | bytes accessed | tf_op | source)
XLA Modules:
  0.0 116.0 jit_solution(16379091209139283387)
XLA Ops:
  0.0 112.8 %update.1 = bf16[32,256,128]{2,1,0:T(8,128)(2,1)} custom-call(bf16[32,256,128]{2,1,0:T(8,128)(2,1)} %pair_ref.1, s32[8,128]{1,0:T(8,128)} %bitcast.5, f32[1,128]{1,0:T(1,128)} %bitcast.6, f32[1,128]{1,0:T(1,128)} %bitcast.7, bf16[128,256]{1,0:T(8,128)(2,1)} %proj_in_hbm.1, bf16[128,256]{1,0:T(8,128)(2,1)} %gate_in_hbm.1, f32[1,128]{1,0:T(1,128)} %bitcast.8, ...), custom_call_target="tpu_custom_call" | custom-call | tf_op jit(solution)/shard_map/update/pallas_call | solution.py:432
  112.8 3.1 %copy.12 = bf16[32,256,128]{2,1,0:T(8,128)(2,1)} copy(bf16[32,256,128]{2,1,0:T(8,128)(2,1)} %update.1) | data formatting | bytes 4194304

commit v5 on v4

--- a/solution.py
+++ b/solution.py
@@ -16,6 +16,34 @@
 LANES = 128
 SPARE = PARTS - 1
 PEERS = 64
+
+
+def mixed_order(offsets):
+    def steps(offset):
+        used = {"x": float(offset[0])}
+        for name, hops in zip("yz", offset[1:3]):
+            used[name + "+"] = float(hops in (1, 2))
+            used[name + "-"] = float(hops in (2, 3))
+        return used
+
+    load = dict.fromkeys(("x", "y+", "y-", "z+", "z-"), 0.0)
+    left, order = list(offsets), []
+    while left:
+
+        def score(offset):
+            total = {k: v + steps(offset)[k] for k, v in load.items()}
+            return max(total.values()) - min(total.values()), -sum(steps(offset).values())
+
+        best = min(left, key=score)
+        left.remove(best)
+        order.append(best)
+        load = {k: v + steps(best)[k] for k, v in load.items()}
+    return order
+
+
+CHIPS = [(n // 16, n // 4 % 4, n % 4) for n in range(1, 32)]
+OTHERS = mixed_order([(0, 0, 0, 1)] + [c + (n,) for c in CHIPS for n in range(2)])
+CHIPS = mixed_order(CHIPS)
 
 
 def norm_rows(values, gain, bias):
@@ -98,13 +126,12 @@
     def group(b2, y2, z2, core2):
         return ((b2 * 4 + y2) * 4 + z2) * 2 + core2
 
-    def peer(t):
-        k = lax.rem(t * 37, PEERS)
+    def peer(offset):
         return (
-            lax.rem(b + lax.div(k, 32), 2),
-            lax.rem(y + lax.rem(lax.div(k, 8), 4), 4),
-            lax.rem(z + lax.rem(lax.div(k, 2), 4), 4),
-            lax.rem(core + lax.rem(k, 2), 2),
+            lax.rem(b + offset[0], 2),
+            lax.rem(y + offset[1], 4),
+            lax.rem(z + offset[2], 4),
+            lax.rem(core + offset[3], 2),
         )
 
     def across(core2):
@@ -134,13 +161,10 @@
 
     barrier = pltpu.get_barrier_semaphore()
 
-    def greet(t, carry):
-        pl.semaphore_signal(barrier, inc=1, device_id=place(*peer(t)), device_id_type=MESH)
-        return carry
-
     for core2 in range(2):
         pl.semaphore_signal(barrier, inc=1, device_id=across(core2), device_id_type=MESH)
-    lax.fori_loop(1, PEERS, greet, 0)
+    for offset in OTHERS:
+        pl.semaphore_signal(barrier, inc=1, device_id=place(*peer(offset)), device_id_type=MESH)
     pl.semaphore_wait(barrier, PEERS + 1)
 
     def rows_for(half2, core2, r):
@@ -218,8 +242,8 @@
         hidden[:, 1, part_rows(r), :] = rounded[1]
         here = pl.ds(pl.multiple_of(r * (8 * STEP) + spot * STEP, STEP), STEP)
 
-        def send_acts(t, inner):
-            to = peer(t)
+        for offset in OTHERS:
+            to = peer(offset)
             pltpu.make_async_remote_copy(
                 src_ref=hidden.at[pl.ds(2 * group(*to), 2), :, part_rows(r), :],
                 dst_ref=acts.at[:, :, col, here, :],
@@ -228,9 +252,6 @@
                 device_id=place(*to),
                 device_id_type=MESH,
             ).start()
-            return inner
-
-        lax.fori_loop(1, PEERS, send_acts, 0)
         pltpu.make_async_copy(
             hidden.at[pl.ds(2 * mine, 2), :, part_rows(r), :], acts.at[:, :, col, here, :], own_act_sem.at[r]
         ).start()
@@ -272,8 +293,8 @@
     extra[...] = stage[pl.ds(0, hids * STEP), :].astype(jnp.bfloat16).reshape(hids, STEP, LANES)
     spare_rows = pl.ds(pl.multiple_of(SPARE * (8 * STEP) + spot * STEP, STEP), STEP)
 
-    def send_extra(t, carry):
-        to = peer(t)
+    for offset in OTHERS:
+        to = peer(offset)
         pltpu.make_async_remote_copy(
             src_ref=extra.at[pl.ds(2 * group(*to), 2)],
             dst_ref=far.at[:, col, spare_rows, :],
@@ -282,9 +303,6 @@
             device_id=place(*to),
             device_id_type=MESH,
         ).start()
-        return carry
-
-    lax.fori_loop(1, PEERS, send_extra, 0)
     pltpu.make_async_copy(
         extra.at[pl.ds(2 * mine, 2)], far.at[:, col, spare_rows, :], own_extra_sem
     ).start()
@@ -293,12 +311,13 @@
         pass_right(r)
     take_acts(SPARE)
 
-    def multiply(turn, load_right):
+    def multiply(turn, start, parts, load_right):
+        rows = pl.ds(start * (8 * STEP), parts * (8 * STEP))
         which = lax.rem(half + turn, 2)
 
         def block(n, carry):
             h, m = lax.div(n, 2), lax.rem(n, 2)
-            left = jnp.concatenate([acts[h, 0, c] for c in range(8)], axis=1)
+            left = jnp.concatenate([acts[h, 0, c, rows, :] for c in range(8)], axis=1)
             right = []
             for c in range(8):
                 right.append(
@@ -319,27 +338,17 @@
                 preferred_element_type=jnp.float32,
             ).astype(jnp.bfloat16)
             for s in range(2):
-                tri[h, (m * 2 + s) * 2 + which] = prod[:, s * LANES : (s + 1) * LANES].reshape(
-                    PARTS, 8 * STEP, LANES
-                )
+                tri[h, (m * 2 + s) * 2 + which, pl.ds(start, parts)] = prod[
+                    :, s * LANES : (s + 1) * LANES
+                ].reshape(parts, 8 * STEP, LANES)
             return carry
 
         lax.fori_loop(0, 4, block, 0)
 
-    multiply(0, lambda h, c, rows: acts[h, 1, c, rows, :])
-    held = extra.at[pl.ds(0, 2 * PEERS - 2)]
-    pltpu.make_async_copy(held, held, extra_sem).wait()
-    held = extra.at[pl.ds(0, 2)]
-    pltpu.make_async_copy(held, held, own_extra_sem).wait()
-    held = far.at[:, :, pl.ds(0, SPARE * 8 * STEP), :]
-    pltpu.make_async_copy(held, held, far_sem).wait()
-    multiply(1, lambda h, c, rows: far[h, c, rows, :])
-
-    def send_round(n, carry):
+    def send_round(n):
         part = pl.ds(n * PER, PER)
 
-        def send_sums(t, inner):
-            b2, y2, z2, core2 = peer(t)
+        def send_sums(b2, y2, z2, core2):
             pltpu.make_async_remote_copy(
                 src_ref=tri.at[
                     :, b2 * 4 + z2, part, pl.ds(pl.multiple_of((y2 * 2 + core2) * STEP, STEP), STEP), :
@@ -350,17 +359,28 @@
                 device_id=place(b2, y2, z2, core2),
                 device_id_type=MESH,
             ).start()
-            return inner
-
-        lax.fori_loop(1, PEERS, send_sums, 0)
+
+        send_sums(b, y, z, 1 - core)
         pltpu.make_async_copy(
             tri.at[:, col, part, pl.ds(pl.multiple_of(spot * STEP, STEP), STEP), :],
             sums.at[pl.ds(2 * mine, 2), part],
             own_sum_sem.at[n],
         ).start()
-        return carry
-
-    lax.fori_loop(0, ROUNDS, send_round, 0)
+        for core2 in range(2):
+            for offset in CHIPS:
+                send_sums(*peer(offset + (0,))[:3], core2)
+
+    multiply(0, 0, PARTS, lambda h, c, rows: acts[h, 1, c, rows, :])
+    held = extra.at[pl.ds(0, 2 * PEERS - 2)]
+    pltpu.make_async_copy(held, held, extra_sem).wait()
+    held = extra.at[pl.ds(0, 2)]
+    pltpu.make_async_copy(held, held, own_extra_sem).wait()
+    held = far.at[:, :, pl.ds(0, SPARE * 8 * STEP), :]
+    pltpu.make_async_copy(held, held, far_sem).wait()
+    for n in range(2):
+        multiply(1, n * (PARTS // 2), PARTS // 2, lambda h, c, rows: far[h, c, rows, :])
+        for m in range(n * (ROUNDS // 2), (n + 1) * (ROUNDS // 2)):
+            send_round(m)
 
     def make_update(r, carry):
         flat[...] = sums[:, r].astype(jnp.float32).reshape(hids * STEP, LANES)
@@ -432,7 +452,7 @@
     return pl.pallas_call(
         kernel,
         name="update",
-        out_shape=jax.ShapeDtypeStruct(pair.shape, jnp.bfloat16),
+        out_shape=pltpu.VMEM(pair.shape, jnp.bfloat16),
         in_specs=[pl.BlockSpec(memory_space=pl.ANY)] + [pl.BlockSpec(memory_space=pl.ANY)] * 9,
         out_specs=pl.BlockSpec(memory_space=pl.ANY),
         scratch_shapes=[

time: 116 us -> 110 us (0.948)
  Pallas kernels: 113 us -> 108 us
  local copies, waits for them, and re-layouts: 3.14 us -> 1.32 us
    pallas_call x1, Pallas kernels: 113 us -> 108 us  [local(): pl.pallas_call(kernel, name='update', out_shape=pltpu.VMEM(pair.shape, jn...]
    unnamed x1, local copies, waits for them, and re-layouts: 3.14 us -> 1.32 us
where the time goes in v5:
time: 110 us; the launch traced here: 109 us
  Pallas kernels  108 us (98%)
  local copies, waits for them, and re-layouts  1.32 us (1%)
    pallas_call x1, Pallas kernels, local(): pl.pallas_call(kernel, name='update', out_shape=pltpu.VMEM(pair.shape, jn...  108 us

profile of v5, /device:TPU:1, one launch (start us, length us, event | category | flops | bytes accessed | tf_op | source)
XLA Modules:
  0.0 109.5 jit_solution(11898907805673104088)
XLA Ops:
  0.0 108.2 %update.1 = bf16[32,256,128]{2,1,0:T(8,128)(2,1)S(1)} custom-call(bf16[32,256,128]{2,1,0:T(8,128)(2,1)} %pair_ref.1, s32[8,128]{1,0:T(8,128)} %bitcast.5, f32[1,128]{1,0:T(1,128)} %bitcast.6, f32[1,128]{1,0:T(1,128)} %bitcast.7, bf16[128,256]{1,0:T(8,128)(2,1)} %proj_in_hbm.1, bf16[128,256]{1,0:T(8,128)(2,1)} %gate_in_hbm.1, f32[1,128]{1,0:T(1,128)} %bitcast.8, ...), custom_call_target="tpu_custom_call" | custom-call | tf_op jit(solution)/shard_map/update/pallas_call | solution.py:452
  108.2 1.3 %copy.12 = bf16[32,256,128]{2,1,0:T(8,128)(2,1)} copy(bf16[32,256,128]{2,1,0:T(8,128)(2,1)S(1)} %update.1) | data formatting | bytes 4194304

commit v6 on v5

--- a/solution.py
+++ b/solution.py
@@ -11,8 +11,7 @@
 MESH = pl.DeviceIdType.MESH
 STEP = 16
 PARTS = 4
-ROUNDS = 4
-PER = PARTS // ROUNDS
+AHEAD = 2
 LANES = 128
 SPARE = PARTS - 1
 PEERS = 64
@@ -54,8 +53,8 @@
     return ((values - center) * lax.rsqrt(spread + epsilon) * gain + bias).astype(jnp.bfloat16)
 
 
-def sigmoid(values):
-    return 0.5 * jnp.tanh(0.5 * values) + 0.5
+def twice_sigmoid(half_values):
+    return jnp.tanh(half_values) + 1.0
 
 
 def part_rows(r):
@@ -88,6 +87,7 @@
     affine,
     weight_in,
     weight_out,
+    ready,
     extra,
     token_ref,
     gain_in_ref,
@@ -153,9 +153,6 @@
             )
         )
     ]
-    for copy in small:
-        copy.start()
-
     mine = group(b, y, z, core)
     spot = y * 2 + core
 
@@ -165,6 +162,8 @@
         pl.semaphore_signal(barrier, inc=1, device_id=across(core2), device_id_type=MESH)
     for offset in OTHERS:
         pl.semaphore_signal(barrier, inc=1, device_id=place(*peer(offset)), device_id_type=MESH)
+    for copy in small:
+        copy.start()
     pl.semaphore_wait(barrier, PEERS + 1)
 
     def rows_for(half2, core2, r):
@@ -193,26 +192,26 @@
     lax.fori_loop(0, PARTS + 1, send_pairs, 0)
 
     chans = pairs.shape[0]
-    hids = hidden.shape[0]
-
-    def turned(ref):
-        return ref[...].astype(jnp.float32).T.astype(jnp.bfloat16)
+    hids = hidden.shape[1]
+
+    def turned(ref, scale=1.0):
+        return (ref[...].astype(jnp.float32).T * scale).astype(jnp.bfloat16)
 
     def column(vec):
         return jnp.broadcast_to(vec, (LANES, LANES)).T
 
     for copy in small:
         copy.wait()
-    weight_in[: 2 * hids] = turned(gate_in_ref)
+    weight_in[: 2 * hids] = turned(gate_in_ref, 0.5)
     weight_in[2 * hids : 4 * hids] = turned(proj_in_ref)
-    weight_in[4 * hids :] = turned(gate_out_ref)
-    weight_out[...] = turned(proj_out_ref)
+    weight_in[4 * hids :] = turned(gate_out_ref, 0.5)
+    weight_out[...] = turned(proj_out_ref, 0.5)
     for n, ref in enumerate((gain_in_ref, bias_in_ref, gain_out_ref, bias_out_ref)):
         affine[n] = column(ref[...])
     for n in range(2):
         mask[n] = column(
             token_ref[pl.ds(y * 2 + lax.rem(half + n, 2), 1), :].astype(jnp.float32)
-        ) * token_ref[pl.ds(col, 1), :].astype(jnp.float32)
+        ) * (token_ref[pl.ds(col, 1), :].astype(jnp.float32) * 0.5)
 
     def take_pairs(r):
         held = pairs.at[pl.ds(0, 3 * chan_part), pl.ds(0, STEP), :]
@@ -227,42 +226,10 @@
         ]
         return jnp.concatenate(both, axis=1)
 
-    def make_hidden(r, carry):
-        take_pairs(r)
-        here_mask = mask[0, pl.ds(pl.multiple_of(core * tall + r * STEP, STEP), STEP), :]
-        for i in range(0, STEP, 2):
-            prod = jnp.dot(weight_in[...], normed(i), preferred_element_type=jnp.float32)
-            for d in range(2):
-                part = prod[:, d * LANES : (d + 1) * LANES]
-                act = sigmoid(part[: 2 * hids]) * part[2 * hids : 4 * hids] * here_mask[i + d : i + d + 1, :]
-                stage[pl.ds(i + d, 2 * hids, stride=STEP), :] = act
-                gates[r * STEP + (i + d)] = sigmoid(part[4 * hids :])
-        rounded = stage[...].astype(jnp.bfloat16).reshape(2, hids, STEP, LANES)
-        hidden[:, 0, part_rows(r), :] = rounded[0]
-        hidden[:, 1, part_rows(r), :] = rounded[1]
-        here = pl.ds(pl.multiple_of(r * (8 * STEP) + spot * STEP, STEP), STEP)
-
-        for offset in OTHERS:
-            to = peer(offset)
-            pltpu.make_async_remote_copy(
-                src_ref=hidden.at[pl.ds(2 * group(*to), 2), :, part_rows(r), :],
-                dst_ref=acts.at[:, :, col, here, :],
-                send_sem=send_sem.at[1],
-                recv_sem=act_sem.at[r],
-                device_id=place(*to),
-                device_id_type=MESH,
-            ).start()
-        pltpu.make_async_copy(
-            hidden.at[pl.ds(2 * mine, 2), :, part_rows(r), :], acts.at[:, :, col, here, :], own_act_sem.at[r]
-        ).start()
-        return carry
-
-    lax.fori_loop(0, PARTS, make_hidden, 0)
-
     def take_acts(r):
-        held = hidden.at[pl.ds(0, 2 * PEERS - 2), :, pl.ds(0, STEP), :]
+        held = hidden.at[0, pl.ds(0, 2 * PEERS - 2)]
         pltpu.make_async_copy(held, held, act_sem.at[r]).wait()
-        held = hidden.at[pl.ds(0, 2), :, pl.ds(0, STEP), :]
+        held = hidden.at[0, pl.ds(0, 2)]
         pltpu.make_async_copy(held, held, own_act_sem.at[r]).wait()
 
     def pass_right(r):
@@ -277,7 +244,42 @@
             device_id_type=MESH,
         ).start()
 
-    pass_right(0)
+    def make_hidden(r, carry):
+        take_pairs(r)
+        here_mask = mask[0, pl.ds(pl.multiple_of(core * tall + r * STEP, STEP), STEP), :]
+        for i in range(0, STEP, 2):
+            prod = jnp.dot(weight_in[...], normed(i), preferred_element_type=jnp.float32)
+            for d in range(2):
+                part = prod[:, d * LANES : (d + 1) * LANES]
+                act = twice_sigmoid(part[: 2 * hids]) * part[2 * hids : 4 * hids] * here_mask[i + d : i + d + 1, :]
+                stage[pl.ds(i + d, 2 * hids, stride=STEP), :] = act
+                gates[r * STEP + (i + d)] = twice_sigmoid(part[4 * hids :])
+        rounded = stage[...].astype(jnp.bfloat16).reshape(2, hids, STEP, LANES)
+        hidden[r, :, 0] = rounded[0]
+        hidden[r, :, 1] = rounded[1]
+        here = pl.ds(pl.multiple_of(r * (8 * STEP) + spot * STEP, STEP), STEP)
+
+        @pl.when(r == PARTS - 1)
+        def _():
+            pass_right(0)
+
+
+        for offset in OTHERS:
+            to = peer(offset)
+            pltpu.make_async_remote_copy(
+                src_ref=hidden.at[r, pl.ds(2 * group(*to), 2)],
+                dst_ref=acts.at[:, :, col, here, :],
+                send_sem=send_sem.at[1],
+                recv_sem=act_sem.at[r],
+                device_id=place(*to),
+                device_id_type=MESH,
+            ).start()
+        pltpu.make_async_copy(
+            hidden.at[r, pl.ds(2 * mine, 2)], acts.at[:, :, col, here, :], own_act_sem.at[r]
+        ).start()
+        return carry
+
+    lax.fori_loop(0, PARTS, make_hidden, 0)
 
     take_pairs(PARTS)
     spare_mask = mask[1, pl.ds(pl.multiple_of(core * tall + SPARE * STEP, STEP), STEP), :]
@@ -288,7 +290,7 @@
         for d in range(2):
             lanes = slice(d * LANES, (d + 1) * LANES)
             stage[pl.ds(i + d, hids, stride=STEP), :] = (
-                sigmoid(gate[:, lanes]) * prod[:, lanes] * spare_mask[i + d : i + d + 1, :]
+                twice_sigmoid(gate[:, lanes]) * prod[:, lanes] * spare_mask[i + d : i + d + 1, :]
             )
     extra[...] = stage[pl.ds(0, hids * STEP), :].astype(jnp.bfloat16).reshape(hids, STEP, LANES)
     spare_rows = pl.ds(pl.multiple_of(SPARE * (8 * STEP) + spot * STEP, STEP), STEP)
@@ -338,22 +340,18 @@
                 preferred_element_type=jnp.float32,
             ).astype(jnp.bfloat16)
             for s in range(2):
-                tri[h, (m * 2 + s) * 2 + which, pl.ds(start, parts)] = prod[
+                tri[(m * 2 + s) * 2 + which, pl.ds(start, parts), :, h] = prod[
                     :, s * LANES : (s + 1) * LANES
-                ].reshape(parts, 8 * STEP, LANES)
+                ].reshape(parts, 8, STEP, LANES)
             return carry
 
         lax.fori_loop(0, 4, block, 0)
 
     def send_round(n):
-        part = pl.ds(n * PER, PER)
-
         def send_sums(b2, y2, z2, core2):
             pltpu.make_async_remote_copy(
-                src_ref=tri.at[
-                    :, b2 * 4 + z2, part, pl.ds(pl.multiple_of((y2 * 2 + core2) * STEP, STEP), STEP), :
-                ],
-                dst_ref=sums.at[pl.ds(2 * mine, 2), part],
+                src_ref=tri.at[b2 * 4 + z2, n, y2 * 2 + core2],
+                dst_ref=sums.at[n, pl.ds(2 * mine, 2)],
                 send_sem=send_sem.at[3],
                 recv_sem=sum_sem.at[n],
                 device_id=place(b2, y2, z2, core2),
@@ -362,8 +360,8 @@
 
         send_sums(b, y, z, 1 - core)
         pltpu.make_async_copy(
-            tri.at[:, col, part, pl.ds(pl.multiple_of(spot * STEP, STEP), STEP), :],
-            sums.at[pl.ds(2 * mine, 2), part],
+            tri.at[col, n, spot],
+            sums.at[n, pl.ds(2 * mine, 2)],
             own_sum_sem.at[n],
         ).start()
         for core2 in range(2):
@@ -379,51 +377,56 @@
     pltpu.make_async_copy(held, held, far_sem).wait()
     for n in range(2):
         multiply(1, n * (PARTS // 2), PARTS // 2, lambda h, c, rows: far[h, c, rows, :])
-        for m in range(n * (ROUNDS // 2), (n + 1) * (ROUNDS // 2)):
-            send_round(m)
+        send_round(n)
 
     def make_update(r, carry):
-        flat[...] = sums[:, r].astype(jnp.float32).reshape(hids * STEP, LANES)
+        held = sums.at[0, pl.ds(0, 2 * PEERS - 2)]
+        pltpu.make_async_copy(held, held, sum_sem.at[r]).wait()
+        held = sums.at[0, pl.ds(0, 2)]
+        pltpu.make_async_copy(held, held, own_sum_sem.at[r]).wait()
+        flat[...] = sums[r].astype(jnp.float32).reshape(hids * STEP, LANES)
         for i in range(0, STEP, 2):
             both = [
                 norm_rows(flat[pl.ds(i + d, hids, stride=STEP), :], affine[2], affine[3])
                 for d in range(2)
             ]
-            prod = jnp.dot(
-                weight_out[...], jnp.concatenate(both, axis=1), preferred_element_type=jnp.float32
+            ready[i // 2] = jnp.concatenate(both, axis=1)
+        rows = pl.ds(pl.multiple_of(quarter * tall + r * STEP, STEP), STEP)
+        share = chans // 2
+        for chip in (1 - low, low):
+            here = pl.ds(pl.multiple_of(chip * share, share), share)
+            weight = weight_out[here, :]
+            for i in range(0, STEP, 2):
+                prod = jnp.dot(weight, ready[i // 2], preferred_element_type=jnp.float32)
+                for d in range(2):
+                    stage[pl.ds(i + d, share, stride=STEP), :] = (
+                        gates[r * STEP + (i + d), here, :] * prod[:, d * LANES : (d + 1) * LANES]
+                    )
+            result[here, part_rows(r), :] = (
+                stage[pl.ds(0, share * STEP), :].astype(jnp.bfloat16).reshape(share, STEP, LANES)
             )
-            for d in range(2):
-                stage[pl.ds(i + d, chans, stride=STEP), :] = (
-                    gates[r * STEP + (i + d)] * prod[:, d * LANES : (d + 1) * LANES]
-                )
-        result[:, part_rows(r), :] = (
-            stage[pl.ds(0, chans * STEP), :].astype(jnp.bfloat16).reshape(chans, STEP, LANES)
-        )
-        rows = pl.ds(pl.multiple_of(quarter * tall + r * STEP, STEP), STEP)
-        for step in range(1, 4):
-            ch2 = lax.rem(ch + step, 4)
-            pltpu.make_async_remote_copy(
-                src_ref=result.at[pl.ds(ch2 * chan_part, chan_part), part_rows(r), :],
-                dst_ref=out_ref.at[:, rows, :],
-                send_sem=send_sem.at[4],
-                recv_sem=out_sem,
-                device_id={"row": y, "col": col, "ch": ch2},
-                device_id_type=MESH,
-            ).start()
+            first = chip is not low
+            for core2 in (0, 1) if first else (1 - core,):
+                ch2 = chip * 2 + core2
+                pltpu.make_async_remote_copy(
+                    src_ref=result.at[pl.ds(ch2 * chan_part, chan_part), part_rows(r), :],
+                    dst_ref=out_ref.at[:, rows, :],
+                    send_sem=send_sem.at[4],
+                    recv_sem=out_sem,
+                    device_id={"row": y, "col": col, "ch": ch2},
+                    device_id_type=MESH,
+                ).start()
         pltpu.make_async_copy(
             result.at[pl.ds(ch * chan_part, chan_part), part_rows(r), :], out_ref.at[:, rows, :], own_out_sem
         ).start()
+
+        @pl.when(r + AHEAD < PARTS)
+        def _():
+            send_round(r + AHEAD)
+
         return carry
 
-    def take_round(n, carry):
-        held = sums.at[pl.ds(0, 2 * PEERS - 2), pl.ds(0, PER)]
-        pltpu.make_async_copy(held, held, sum_sem.at[n]).wait()
-        held = sums.at[pl.ds(0, 2), pl.ds(0, PER)]
-        pltpu.make_async_copy(held, held, own_sum_sem.at[n]).wait()
-        lax.fori_loop(n * PER, n * PER + PER, make_update, 0)
-        return carry
-
-    lax.fori_loop(0, ROUNDS, take_round, 0)
+    lax.fori_loop(0, PARTS, make_update, 0)
 
     held = result.at[pl.ds(0, 3 * chan_part)]
     pltpu.make_async_copy(held, held, out_sem).wait()
@@ -432,9 +435,9 @@
     for n, held in enumerate(
         (
             pairs.at[pl.ds(0, 3 * chan_part)],
-            hidden.at[pl.ds(0, 2 * PEERS - 2)],
+            hidden.at[:, pl.ds(0, 2 * PEERS - 2)],
             far.at[:, :, pl.ds(0, SPARE * 8 * STEP), :],
-            sums.at[pl.ds(0, 2 * PEERS - 2)],
+            sums.at[:, pl.ds(0, 2 * PEERS - 2)],
             result.at[pl.ds(0, 3 * chan_part)],
             extra.at[pl.ds(0, 2 * PEERS - 2)],
         )
@@ -457,12 +460,12 @@
         out_specs=pl.BlockSpec(memory_space=pl.ANY),
         scratch_shapes=[
             half16(chans, tall + STEP, lanes),
-            half16(hids, 2, tall, lanes),
+            half16(PARTS, hids, 2, STEP, lanes),
             pltpu.VMEM((tall, chans, lanes), jnp.float32),
             half16(2, 2, 8, PARTS * 8 * STEP, lanes),
             half16(2, 8, PARTS * 8 * STEP, lanes),
-            half16(2, 8, PARTS, 8 * STEP, lanes),
-            half16(hids, PARTS, STEP, lanes),
+            half16(8, PARTS, 8, 2, STEP, lanes),
+            half16(PARTS, hids, STEP, lanes),
             half16(chans, tall, lanes),
             pltpu.VMEM((chans * STEP, lanes), jnp.float32),
             pltpu.VMEM((2 * hids * STEP, lanes), jnp.float32),
@@ -470,6 +473,7 @@
             pltpu.VMEM((4, lanes, lanes), jnp.float32),
             half16(4 * hids + chans, chans),
             half16(chans, hids),
+            half16(STEP // 2, hids, 2 * lanes),
             half16(hids, STEP, lanes),
             pltpu.VMEM((token_mask.shape[0] // lanes, lanes), jnp.int32),
             pltpu.VMEM((1, lanes), jnp.float32),
@@ -485,12 +489,12 @@
             dma((PARTS,)),
             dma,
             dma,
-            dma((ROUNDS,)),
+            dma((PARTS,)),
             dma,
             dma((PARTS + 1,)),
             dma((PARTS,)),
             dma,
-            dma((ROUNDS,)),
+            dma((PARTS,)),
             dma,
             dma((9,)),
         ],

time: 110 us -> 110 us (level)
  no operation moved by 1% of the time
where the time goes in v6:
time: 110 us; the launch traced here: 109 us
  Pallas kernels  108 us (98%)
  local copies, waits for them, and re-layouts  1.32 us (1%)
    pallas_call x1, Pallas kernels, local(): pl.pallas_call(kernel, name='update', out_shape=pltpu.VMEM(pair.shape, jn...  108 us

profile of v6, /device:TPU:1, one launch (start us, length us, event | category | flops | bytes accessed | tf_op | source)
XLA Modules:
  0.0 109.5 jit_solution(17203016480652541936)
XLA Ops:
  0.0 108.2 %update.1 = bf16[32,256,128]{2,1,0:T(8,128)(2,1)S(1)} custom-call(bf16[32,256,128]{2,1,0:T(8,128)(2,1)} %pair_ref.1, s32[8,128]{1,0:T(8,128)} %bitcast.5, f32[1,128]{1,0:T(1,128)} %bitcast.6, f32[1,128]{1,0:T(1,128)} %bitcast.7, bf16[128,256]{1,0:T(8,128)(2,1)} %proj_in_hbm.1, bf16[128,256]{1,0:T(8,128)(2,1)} %gate_in_hbm.1, f32[1,128]{1,0:T(1,128)} %bitcast.8, ...), custom_call_target="tpu_custom_call" | custom-call | tf_op jit(solution)/shard_map/update/pallas_call | solution.py:455
  108.2 1.3 %copy.12 = bf16[32,256,128]{2,1,0:T(8,128)(2,1)} copy(bf16[32,256,128]{2,1,0:T(8,128)(2,1)S(1)} %update.1) | data formatting | bytes 4194304

commit v7 on v6

--- a/solution.py
+++ b/solution.py
@@ -375,8 +375,8 @@
     pltpu.make_async_copy(held, held, own_extra_sem).wait()
     held = far.at[:, :, pl.ds(0, SPARE * 8 * STEP), :]
     pltpu.make_async_copy(held, held, far_sem).wait()
-    for n in range(2):
-        multiply(1, n * (PARTS // 2), PARTS // 2, lambda h, c, rows: far[h, c, rows, :])
+    for n, parts in enumerate((1, PARTS - 1)):
+        multiply(1, n, parts, lambda h, c, rows: far[h, c, rows, :])
         send_round(n)
 
     def make_update(r, carry):

time: 110 us -> 109 us (level)
  no operation moved by 1% of the time
where the time goes in v7:
time: 109 us
  Pallas kernels  108 us (99%)
  local copies, waits for them, and re-layouts  1.32 us (1%)
    pallas_call x1, Pallas kernels, local(): pl.pallas_call(kernel, name='update', out_shape=pltpu.VMEM(pair.shape, jn...  108 us

profile of v7, /device:TPU:1, one launch (start us, length us, event | category | flops | bytes accessed | tf_op | source)
XLA Modules:
  0.0 109.4 jit_solution(12795845235461680969)
XLA Ops:
  0.0 108.0 %update.1 = bf16[32,256,128]{2,1,0:T(8,128)(2,1)S(1)} custom-call(bf16[32,256,128]{2,1,0:T(8,128)(2,1)} %pair_ref.1, s32[8,128]{1,0:T(8,128)} %bitcast.5, f32[1,128]{1,0:T(1,128)} %bitcast.6, f32[1,128]{1,0:T(1,128)} %bitcast.7, bf16[128,256]{1,0:T(8,128)(2,1)} %proj_in_hbm.1, bf16[128,256]{1,0:T(8,128)(2,1)} %gate_in_hbm.1, f32[1,128]{1,0:T(1,128)} %bitcast.8, ...), custom_call_target="tpu_custom_call" | custom-call | tf_op jit(solution)/shard_map/update/pallas_call | solution.py:455
  108.1 1.3 %copy.12 = bf16[32,256,128]{2,1,0:T(8,128)(2,1)} copy(bf16[32,256,128]{2,1,0:T(8,128)(2,1)S(1)} %update.1) | data formatting | bytes 4194304

commit v8 on v6

--- a/solution.py
+++ b/solution.py
@@ -11,7 +11,7 @@
 MESH = pl.DeviceIdType.MESH
 STEP = 16
 PARTS = 4
-AHEAD = 2
+AHEAD = 3
 LANES = 128
 SPARE = PARTS - 1
 PEERS = 64
@@ -378,6 +378,7 @@
     for n in range(2):
         multiply(1, n * (PARTS // 2), PARTS // 2, lambda h, c, rows: far[h, c, rows, :])
         send_round(n)
+    send_round(AHEAD - 1)
 
     def make_update(r, carry):
         held = sums.at[0, pl.ds(0, 2 * PEERS - 2)]

time: 110 us -> 110 us (level)
  no operation moved by 1% of the time
where the time goes in v8:
time: 110 us
  Pallas kernels  108 us (98%)
  local copies, waits for them, and re-layouts  1.32 us (1%)
    pallas_call x1, Pallas kernels, local(): pl.pallas_call(kernel, name='update', out_shape=pltpu.VMEM(pair.shape, jn...  108 us

profile of v8, /device:TPU:1, one launch (start us, length us, event | category | flops | bytes accessed | tf_op | source)
XLA Modules:
  0.0 109.5 jit_solution(357966562525776008)
XLA Ops:
  0.0 108.2 %update.1 = bf16[32,256,128]{2,1,0:T(8,128)(2,1)S(1)} custom-call(bf16[32,256,128]{2,1,0:T(8,128)(2,1)} %pair_ref.1, s32[8,128]{1,0:T(8,128)} %bitcast.5, f32[1,128]{1,0:T(1,128)} %bitcast.6, f32[1,128]{1,0:T(1,128)} %bitcast.7, bf16[128,256]{1,0:T(8,128)(2,1)} %proj_in_hbm.1, bf16[128,256]{1,0:T(8,128)(2,1)} %gate_in_hbm.1, f32[1,128]{1,0:T(1,128)} %bitcast.8, ...), custom_call_target="tpu_custom_call" | custom-call | tf_op jit(solution)/shard_map/update/pallas_call | solution.py:456
  108.2 1.3 %copy.12 = bf16[32,256,128]{2,1,0:T(8,128)(2,1)} copy(bf16[32,256,128]{2,1,0:T(8,128)(2,1)S(1)} %update.1) | data formatting | bytes 4194304
